TPU v7x, 32 devices: a whole 2x2x4 slice. The times are simulated.
32 devices in a mesh: dp: 8 (over z, x), tensor: 4 (over y, core).
Axes of the slice: x: 2, y: 2, z: 4, core: 2. Of those that a mesh axis runs over, the one named last changes fastest.
Arguments:
- block_input: bfloat16 [8, 2048, 1024], P('dp', 'tensor'), may hold values from -6 to 6
- segment_ids: int32 [8, 2048], P('dp', 'tensor'), may hold values from 0 to 3, as said below
- w_qkv: bfloat16 [3, 1024, 1024], P(None, None, 'tensor'), may hold values from -0.1875 to 0.1875
- w_out: bfloat16 [1024, 1024], P('tensor'), may hold values from -0.75 to 0.75
- w_up: bfloat16 [1024, 4096], P(None, 'tensor'), may hold values from -0.1875 to 0.1875
- w_down: bfloat16 [4096, 1024], P('tensor'), may hold values from -0.09375 to 0.09375
- ln1_gain: float32 [1024], replicated, may hold values from 0.5 to 1.5
- ln1_bias: float32 [1024], replicated, may hold values from -1 to 1
- ln2_gain: float32 [1024], replicated, may hold values from 0.5 to 1.5
- ln2_bias: float32 [1024], replicated, may hold values from -1 to 1
- out_bias: float32 [1024], replicated, may hold values from -1 to 1
- down_bias: float32 [1024], replicated, may hold values from -1 to 1
- cotangent: bfloat16 [8, 2048, 1024], P('dp', 'tensor'), may hold values from -6 to 6
Outputs:
- block_output: bfloat16 [8, 2048, 1024], P('dp', 'tensor')
- x_grad: float32 [8, 2048, 1024], P('dp', 'tensor')
- w_qkv_grad: float32 [3, 1024, 1024], P(None, 'dp', 'tensor')
- w_out_grad: float32 [1024, 1024], P('tensor', 'dp')
- w_up_grad: float32 [1024, 4096], P('dp', 'tensor')
- w_down_grad: float32 [4096, 1024], P('tensor', 'dp')
- ln1_gain_grad: float32 [1024], P(('dp', 'tensor'))
- ln1_bias_grad: float32 [1024], P(('dp', 'tensor'))
- ln2_gain_grad: float32 [1024], P(('dp', 'tensor'))
- ln2_bias_grad: float32 [1024], P(('dp', 'tensor'))
- out_bias_grad: float32 [1024], P(('dp', 'tensor'))
- down_bias_grad: float32 [1024], P(('dp', 'tensor'))
Inputs may be any that keep to these rules, and one draw needn't show every extreme that they name: `segment_ids`: in every row the ids run 1, 2, 3 in order and then 0 for padding to the row's end; article 1 holds the first 1 to 256 slots, article 2 ends in the last eighth of the row, and every row has at least one padding slot.
All inputs are finite; a program needn't handle non-finite values.
Results may differ from a plain program's by a relative error of at most 0.018.
Values may be sent and summed in bfloat16 or wider, within the bound.
No kernel may reach another device: no remote copies, remote signals or barrier semaphores. Data moves between devices by JAX's collectives and lax.ppermute only.
A program may use at most 192 MiB of HBM per device.

v0:
```python
import jax
import jax.numpy as jnp
from jax import lax
from jax.sharding import PartitionSpec as P

H = 8
HD = 128


EPS = 1e-05
NEG = -1e30


def layer_norm(values, gain, shift):
    center = values - jnp.mean(values, -1, keepdims=True)
    spread = jnp.mean(center * center, -1, keepdims=True)
    return center * lax.rsqrt(spread + EPS) * gain + shift


def gelu_smooth(values):
    return jax.nn.gelu(values, approximate=True)


def block_scores(queries, keys, seg_query, seg_key, start, slopes):
    count = queries.shape[0]
    scale = queries.shape[-1] ** (-0.5)
    raw = jnp.einsum("qhd,khd->hqk", queries, keys, preferred_element_type=jnp.float32) * scale
    query_place = start + jnp.arange(count, dtype=jnp.int32)
    key_place = jnp.arange(keys.shape[0], dtype=jnp.int32)
    distance = (query_place[:, None] - key_place[None, :]).astype(jnp.float32)
    allowed = (seg_query[:, None] == seg_key[None, :]) & (
        key_place[None, :] <= query_place[:, None]
    )
    return jnp.where(allowed[None], raw - slopes[:, None, None] * distance[None], NEG)


def pick_block(array, index, blocks, size):
    whole_row = lax.dynamic_index_in_dim(array, index // blocks, 0, keepdims=False)
    return lax.dynamic_slice_in_dim(whole_row, index % blocks * size, size, 0)


def pick_row(array, index, blocks):
    return lax.dynamic_index_in_dim(array, index // blocks, 0, keepdims=False)


def local(
    block_input,
    segment_ids,
    w_qkv,
    w_out,
    w_up,
    w_down,
    ln1_gain,
    ln1_bias,
    ln2_gain,
    ln2_bias,
    out_bias,
    down_bias,
    cotangent,
):
    rows = block_input.shape[0]
    local_width = w_qkv.shape[2]
    local_heads = local_width // HD
    x_float = block_input.astype(jnp.float32)
    normed_one = layer_norm(x_float, ln1_gain, ln1_bias)
    gathered = (
        lax.all_gather(normed_one.astype(jnp.bfloat16), "tensor", axis=1, tiled=True),
        lax.all_gather(segment_ids.astype(jnp.bfloat16), "tensor", axis=1, tiled=True),
    )
    inputs_full = gathered[0]
    segments = gathered[1].astype(jnp.int32)
    length = inputs_full.shape[1]
    size = min(512, length)
    blocks = length // size
    projected = jnp.einsum(
        "rld,cde->crle", inputs_full, w_qkv, preferred_element_type=jnp.float32
    ).astype(jnp.bfloat16)
    shaped = projected.reshape(3, rows, length, local_heads, HD)
    queries, keys, values = (shaped[0], shaped[1], shaped[2])
    first_head = lax.axis_index("tensor") * local_heads
    slopes = jnp.exp2(
        -8.0 * (first_head + 1 + jnp.arange(local_heads, dtype=jnp.int32)).astype(jnp.float32) / H
    )
    indices = jnp.arange(rows * blocks, dtype=jnp.int32)

    def attend(index):
        start = index % blocks * size
        query_block = pick_block(queries, index, blocks, size)
        seg_query = pick_block(segments, index, blocks, size)
        scores = block_scores(
            query_block,
            pick_row(keys, index, blocks),
            seg_query,
            pick_row(segments, index, blocks),
            start,
            slopes,
        )
        row_max = jnp.max(scores, -1, keepdims=True)
        exponent = jnp.exp(scores - row_max)
        total = jnp.sum(exponent, -1, keepdims=True)
        weights = (exponent / total).astype(jnp.bfloat16)
        result = jnp.einsum(
            "hqk,khd->qhd",
            weights,
            pick_row(values, index, blocks),
            preferred_element_type=jnp.float32,
        )
        return (result.astype(jnp.bfloat16), row_max[..., 0] + jnp.log(total[..., 0]))

    mixed_blocks, log_totals = lax.map(attend, indices)
    mixed = mixed_blocks.reshape(rows, length, local_width)
    attn_part = jnp.einsum("rle,ed->rld", mixed, w_out, preferred_element_type=jnp.float32)
    attn_sum = lax.psum_scatter(
        attn_part.astype(jnp.bfloat16), "tensor", scatter_dimension=1, tiled=True
    ).astype(jnp.float32)
    resid = x_float + attn_sum + out_bias
    normed_two = layer_norm(resid, ln2_gain, ln2_bias)
    normed_low = normed_two.astype(jnp.bfloat16)
    ffn_input = lax.all_gather(normed_low, "tensor", axis=1, tiled=True)
    up_matrix, down_matrix = (w_up, w_down)
    pre_act = jnp.einsum("rld,df->rlf", ffn_input, up_matrix, preferred_element_type=jnp.float32)
    activated, gelu_back = jax.vjp(gelu_smooth, pre_act)
    act_low = activated.astype(jnp.bfloat16)
    ffn_part = jnp.einsum("rlf,fd->rld", act_low, down_matrix, preferred_element_type=jnp.float32)
    ffn_out = lax.psum_scatter(
        ffn_part.astype(jnp.bfloat16), "tensor", scatter_dimension=1, tiled=True
    ).astype(jnp.float32)
    valid = (segment_ids != 0).astype(jnp.float32)[..., None]
    output = (valid * (resid + ffn_out + down_bias)).astype(jnp.bfloat16)
    grad_out = valid * cotangent.astype(jnp.float32)
    down_bias_grad = jnp.sum(grad_out, (0, 1))
    grad_low = grad_out.astype(jnp.bfloat16)
    grad_rows = lax.all_gather(grad_low, "tensor", axis=1, tiled=True)
    grad_act = jnp.einsum("rld,fd->rlf", grad_rows, down_matrix, preferred_element_type=jnp.float32)
    down_grad = jnp.einsum("rlf,rld->fd", act_low, grad_rows, preferred_element_type=jnp.float32)
    grad_pre = gelu_back(grad_act)[0].astype(jnp.bfloat16)
    up_grad = jnp.einsum("rld,rlf->df", ffn_input, grad_pre, preferred_element_type=jnp.float32)
    grad_normed = jnp.einsum("rlf,df->rld", grad_pre, up_matrix, preferred_element_type=jnp.float32)
    grad_normed = lax.psum_scatter(
        grad_normed.astype(jnp.bfloat16), "tensor", scatter_dimension=1, tiled=True
    ).astype(jnp.float32)
    norm_two_unused, norm_two_back = jax.vjp(layer_norm, resid, ln2_gain, ln2_bias)
    resid_extra, gain_two_grad, shift_two_grad = norm_two_back(grad_normed)
    grad_resid = grad_out + resid_extra
    out_bias_grad = jnp.sum(grad_resid, (0, 1))
    grad_mixed_rows = lax.all_gather(grad_resid.astype(jnp.bfloat16), "tensor", axis=1, tiled=True)
    grad_mixed = jnp.einsum(
        "rld,ed->rle", grad_mixed_rows, w_out, preferred_element_type=jnp.float32
    ).astype(jnp.bfloat16)
    out_grad = jnp.einsum("rle,rld->ed", mixed, grad_mixed_rows, preferred_element_type=jnp.float32)
    grad_heads = grad_mixed.reshape(rows, length, local_heads, HD)
    scale = HD ** (-0.5)

    def backward_step(carry, index):
        key_grads, value_grads = carry
        row = index // blocks
        start = index % blocks * size
        query_block = pick_block(queries, index, blocks, size)
        seg_query = pick_block(segments, index, blocks, size)
        key_row = pick_row(keys, index, blocks)
        value_row = pick_row(values, index, blocks)
        grad_block = pick_block(grad_heads, index, blocks, size)
        scores = block_scores(
            query_block, key_row, seg_query, pick_row(segments, index, blocks), start, slopes
        )
        probs = jnp.exp(scores - log_totals[index][..., None])
        grad_probs = jnp.einsum(
            "qhd,khd->hqk", grad_block, value_row, preferred_element_type=jnp.float32
        )
        grad_scores = (
            probs * (grad_probs - jnp.sum(grad_probs * probs, -1, keepdims=True))
        ).astype(jnp.bfloat16)
        query_grad = (
            jnp.einsum("hqk,khd->qhd", grad_scores, key_row, preferred_element_type=jnp.float32)
            * scale
        )
        key_part = (
            jnp.einsum("hqk,qhd->khd", grad_scores, query_block, preferred_element_type=jnp.float32)
            * scale
        )
        value_part = jnp.einsum(
            "hqk,qhd->khd",
            probs.astype(jnp.bfloat16),
            grad_block,
            preferred_element_type=jnp.float32,
        )
        key_grads = key_grads.at[row].add(key_part)
        value_grads = value_grads.at[row].add(value_part)
        return ((key_grads, value_grads), query_grad)

    empty = jnp.zeros((rows, length, local_heads, HD), jnp.float32)
    accumulated, query_grads = lax.scan(backward_step, (empty, empty), indices)
    stacked = jnp.stack(
        [
            query_grads.reshape(rows, length, local_width),
            accumulated[0].reshape(rows, length, local_width),
            accumulated[1].reshape(rows, length, local_width),
        ]
    ).astype(jnp.bfloat16)
    qkv_grad = jnp.einsum("rld,crle->cde", inputs_full, stacked, preferred_element_type=jnp.float32)
    grad_inputs = jnp.einsum("crle,cde->rld", stacked, w_qkv, preferred_element_type=jnp.float32)
    grad_inputs = lax.psum_scatter(
        grad_inputs.astype(jnp.bfloat16), "tensor", scatter_dimension=1, tiled=True
    ).astype(jnp.float32)
    norm_one_unused, norm_one_back = jax.vjp(layer_norm, x_float, ln1_gain, ln1_bias)
    input_extra, gain_one_grad, shift_one_grad = norm_one_back(grad_inputs)
    input_grad = grad_resid + input_extra
    qkv_grad, out_grad, up_grad, down_grad = (
        lax.psum_scatter(qkv_grad, "dp", scatter_dimension=1, tiled=True),
        lax.psum_scatter(out_grad, "dp", scatter_dimension=1, tiled=True),
        lax.psum_scatter(up_grad, "dp", scatter_dimension=0, tiled=True),
        lax.psum_scatter(down_grad, "dp", scatter_dimension=1, tiled=True),
    )
    vectors = (
        lax.psum_scatter(gain_one_grad, ("dp", "tensor"), scatter_dimension=0, tiled=True),
        lax.psum_scatter(shift_one_grad, ("dp", "tensor"), scatter_dimension=0, tiled=True),
        lax.psum_scatter(gain_two_grad, ("dp", "tensor"), scatter_dimension=0, tiled=True),
        lax.psum_scatter(shift_two_grad, ("dp", "tensor"), scatter_dimension=0, tiled=True),
        lax.psum_scatter(out_bias_grad, ("dp", "tensor"), scatter_dimension=0, tiled=True),
        lax.psum_scatter(down_bias_grad, ("dp", "tensor"), scatter_dimension=0, tiled=True),
    )
    return (
        output,
        input_grad,
        qkv_grad,
        out_grad,
        up_grad,
        down_grad,
        vectors[0],
        vectors[1],
        vectors[2],
        vectors[3],
        vectors[4],
        vectors[5],
    )


def solution(mesh):
    in_specs = (
        P("dp", "tensor", None),
        P("dp", "tensor"),
        P(None, None, "tensor"),
        P("tensor", None),
        P(None, "tensor"),
        P("tensor", None),
        P(),
        P(),
        P(),
        P(),
        P(),
        P(),
        P("dp", "tensor", None),
    )
    out_specs = (
        P("dp", "tensor", None),
        P("dp", "tensor", None),
        P(None, "dp", "tensor"),
        P("tensor", "dp"),
        P("dp", "tensor"),
        P("tensor", "dp"),
        P(("dp", "tensor")),
        P(("dp", "tensor")),
        P(("dp", "tensor")),
        P(("dp", "tensor")),
        P(("dp", "tensor")),
        P(("dp", "tensor")),
    )
    return jax.shard_map(local, mesh=mesh, in_specs=in_specs, out_specs=out_specs, check_vma=False)
```

profile of v0, /device:TPU:0, one launch (start us, length us, event | category | flops | bytes accessed | tf_op | source)
XLA Modules:
  0.0 962.9 jit_solution(4013779672506317633)
XLA Ops:
  14.4 6.1 all_gather.15
  20.6 31.1 %all-gather.5.cloned.1.call-done = bf16[1,2048,1024]{2,1,0:T(8,128)(2,1)} async-done(((bf16[1,512,1024]{2,1,0:T(8,128)(2,1)}), bf16[1,2048,1024]{2,1,0:T(8,128)(2,1)}) %all-gather.5.cloned.1.call-update) | async-done | bytes 4194320 | tf_op jit(solution)/shard_map/all_gather | solution.py:67
  51.7 6.1 fusion.76
  64.7 65.9 %while.34 = (s32[]{:T(128)}, bf16[4,512,2,128]{3,2,1,0:T(2,128)(2,1)}, f32[4,2,512]{2,1,0:T(2,128)S(1)}, s32[4]{0:T(128)S(1)}, s32[1,2048]{1,0:T(1,128)S(1)}, /*...) while((s32[]{:T(128)}, ...), condition=%wide.region_5.6_spmd.clone, body=%wide.region_2.5_spmd.clone.sunk | while | flops 1116864000 | bytes 53531024 | solution.py:110
  75.9 4.2 fusion.146
  92.4 4.2 fusion.146
  108.8 4.2 fusion.146
  125.3 4.2 fusion.146
  131.6 4.6 convert_bitcast_fusion.2
  136.5 44.4 %reduce-scatter.9.cloned.1.call-done = bf16[1,512,1024]{2,1,0:T(8,128)(2,1)} async-done(((bf16[1,2048,1024]{2,1,0:T(8,128)(2,1)}), bf16[1,512,1024]{2,1,0:T(8,128)(2,1)}) %reduce-scatter.9.cloned.1.call-update) | async-done | bytes 1048592 | tf_op jit(solution)/shard_map/reduce_scatter | solution.py:113
  188.7 32.1 %all-gather.7.cloned.1.call-done = bf16[1,2048,1024]{2,1,0:T(8,128)(2,1)} async-done(((bf16[1,512,1024]{2,1,0:T(8,128)(2,1)}), bf16[1,2048,1024]{2,1,0:T(8,128)(2,1)}) %all-gather.7.cloned.1.call-update) | async-done | bytes 4194320 | tf_op jit(solution)/shard_map/all_gather | solution.py:119
  220.7 8.9 fusion.62
  229.7 27.6 %all-gather.9.cloned.1.call-done = bf16[1,2048,1024]{2,1,0:T(8,128)(2,1)} async-done(((bf16[1,512,1024]{2,1,0:T(8,128)(2,1)}), bf16[1,2048,1024]{2,1,0:T(8,128)(2,1)}) %all-gather.9.cloned.1.call-update) | async-done | bytes 4194320 | tf_op jit(solution)/shard_map/all_gather | solution.py:133
  257.3 12.5 %fusion.51 = bf16[2048,1024]{1,0:T(8,128)(2,1)S(1)} fusion(f32[2048,1024]{1,0:T(8,128)} %fusion.62, bf16[1024,1024]{1,0:T(8,128)(2,1)} %param.26, bf16[1,2048,1024]{2,1,0:T(8,128)(2,1)} %all-gather.9.cloned.1.call-done), kind=kOutput, calls=%fused_computation.71 | convolution fusion | flops 4336910336 | bytes 18874368 | tf_op jit(solution)/shard_map/rld,fd->rlf/dot_general | solution.py:134
  271.7 6.3 convert_bitcast_fusion
  279.7 10.9 %convert_bitcast_fusion.1 = bf16[1,2048,1024]{2,1,0:T(8,128)(2,1)} fusion(bf16[1024,1024]{1,0:T(8,128)(2,1)S(1)} %copy-done.38, f32[2048,1024]{1,0:T(8,128)} %fusion.62), kind=kOutput, calls=%fused_computation.91 | convolution fusion | flops 4315938816 | bytes 14680064 | tf_op jit(solution)/shard_map/rlf,fd->rld/dot_general | solution.py:124
  290.6 32.2 %reduce-scatter.13.cloned.1.call-done = bf16[1,512,1024]{2,1,0:T(8,128)(2,1)} async-done(((bf16[1,2048,1024]{2,1,0:T(8,128)(2,1)}), bf16[1,512,1024]{2,1,0:T(8,128)(2,1)}) %reduce-scatter.13.cloned.1.call-update) | async-done | bytes 1048592 | tf_op jit(solution)/shard_map/reduce_scatter | solution.py:139
  328.7 41.0 %reduce-scatter.11.cloned.1.call-done = bf16[1,512,1024]{2,1,0:T(8,128)(2,1)} async-done(((bf16[1,2048,1024]{2,1,0:T(8,128)(2,1)}), bf16[1,512,1024]{2,1,0:T(8,128)(2,1)}) %reduce-scatter.11.cloned.1.call-update) | async-done | bytes 1048592 | tf_op jit(solution)/shard_map/reduce_scatter | solution.py:125
  369.7 4.3 fusion.113
  376.7 34.4 %all-gather.11.cloned.1.call-done = bf16[1,2048,1024]{2,1,0:T(8,128)(2,1)} async-done(((bf16[1,512,1024]{2,1,0:T(8,128)(2,1)}), bf16[1,2048,1024]{2,1,0:T(8,128)(2,1)}) %all-gather.11.cloned.1.call-update) | async-done | bytes 4194320 | tf_op jit(solution)/shard_map/all_gather | solution.py:146
  411.1 4.4 fusion.81
  415.6 148.4 %while.35 = (s32[]{:T(128)}, f32[1,2048,2,128]{1,3,2,0:T(8,128)}, f32[1,2048,2,128]{1,3,2,0:T(8,128)}, bf16[4,512,2,128]{3,1,2,0:T(8,128)(2,1)}, s32[4]{0:T(128)...) while((s32[]{:T(128)}, f32[1,2048,2,128]{1,3,2,0:T(8,128)}, ...), condition=%wide.region_16.17_spmd.clone, body=%wide.region_13.16_spmd.clone.sunk | while | flops 2716466688 | bytes 170436336 | solution.py:192
  429.7 5.8 multiply_reduce_fusion.3
  435.5 8.6 multiply_convert_fusion.6
  444.1 4.3 fusion.156
  459.5 4.1 subtract_exponential_fusion.3
  466.8 5.8 multiply_reduce_fusion.3
  472.6 8.6 multiply_convert_fusion.6
  481.3 4.3 fusion.156
  496.6 4.1 subtract_exponential_fusion.3
  503.9 5.8 multiply_reduce_fusion.3
  509.7 8.6 multiply_convert_fusion.6
  518.4 4.3 fusion.156
  533.7 4.1 subtract_exponential_fusion.3
  541.0 5.8 multiply_reduce_fusion.3
  546.8 8.6 multiply_convert_fusion.6
  555.4 4.3 fusion.156
  572.8 7.7 fusion.98
  580.6 6.4 fusion.71
  587.1 10.2 %fusion.60 = f32[1024,1024]{1,0:T(8,128)} fusion(bf16[2048,1024]{1,0:T(8,128)(2,1)} %copy-done.41, bf16[1,2048,1024]{2,1,0:T(8,128)(2,1)} %all-gather.7.cloned.1.call-done), kind=kOutput, calls=%fused_computation.82 | convolution fusion | flops 4294967296 | bytes 12582912 | tf_op jit(solution)/shard_map/rld,rlf->df/dot_general | solution.py:137
  597.6 12.2 %fusion.56 = f32[1024,1024]{1,0:T(8,128)} fusion(bf16[1,2048,1024]{2,1,0:T(8,128)(2,1)} %all-gather.9.cloned.1.call-done, f32[2048,1024]{1,0:T(8,128)} %fusion.62), kind=kOutput, calls=%fused_computation.78 | convolution fusion | flops 4313841664 | bytes 16777216 | tf_op jit(solution)/shard_map/rlf,rld->fd/dot_general | solution.py:135
  611.1 4.5 fusion.52
  615.6 40.2 %reduce-scatter.17.cloned.1.call-done = f32[3,128,256]{1,2,0:T(8,128)} async-done(((f32[3,1024,256]{1,2,0:T(8,128)}), f32[3,128,256]{1,2,0:T(8,128)}) %reduce-scatter.17.cloned.1.call-update) | async-done | bytes 393232 | tf_op jit(solution)/shard_map/reduce_scatter | solution.py:209
  657.7 44.4 %reduce-scatter.15.cloned.1.call-done = bf16[1,512,1024]{2,1,0:T(8,128)(2,1)} async-done(((bf16[1,2048,1024]{2,1,0:T(8,128)(2,1)}), bf16[1,512,1024]{2,1,0:T(8,128)(2,1)}) %reduce-scatter.15.cloned.1.call-update) | async-done | bytes 1048592 | tf_op jit(solution)/shard_map/reduce_scatter | solution.py:202
  706.7 42.0 %all-reduce.6 = (f32[1024]{0:T(1024)S(1)}, f32[1024]{0:T(1024)S(1)}, f32[1024]{0:T(1024)S(1)}, f32[1024]{0:T(1024)S(1)}, f32[1024]{0:T(1024)S(1)}, /*index=5*/f32[1024]{0:T(1024)S(1)}) all-reduce(f32[1024]{0:T(1024)S(1)} %get-tuple-element.474, ...), channel_id=10, replica_groups=mesh['dp'=8,'tensor'=4] {'dp','tensor'}, use_global_device_ids=true, to_apply=%region_25.26.clone | all-reduce | flops 6144 | bytes 49152
  756.1 39.0 %reduce-scatter.21.cloned.1.call-done = f32[128,1024]{1,0:T(8,128)} async-done(((f32[1024,1024]{1,0:T(8,128)}), f32[128,1024]{1,0:T(8,128)}) %reduce-scatter.21.cloned.1.call-update) | async-done | bytes 524304 | tf_op jit(solution)/shard_map/reduce_scatter | solution.py:211
  795.2 92.9 %reduce-scatter.23.cloned.1.call-done = f32[1024,128]{1,0:T(8,128)} async-done(((f32[1024,1024]{1,0:T(8,128)}), f32[1024,128]{1,0:T(8,128)}) %reduce-scatter.23.cloned.1.call-update) | async-done | bytes 524304 | tf_op jit(solution)/shard_map/reduce_scatter | solution.py:212
  888.1 67.6 %reduce-scatter.19.cloned.1.call-done = f32[256,128]{1,0:T(8,128)} async-done(((f32[256,1024]{1,0:T(8,128)}), f32[256,128]{1,0:T(8,128)}) %reduce-scatter.19.cloned.1.call-update) | async-done | bytes 131088 | tf_op jit(solution)/shard_map/reduce_scatter | solution.py:210
  (279 shorter events, 145.6 us)
Async XLA Ops:
  7.2 213.6 %copy-start = (bf16[1024,1024]{1,0:T(8,128)(2,1)S(1)}, bf16[1024,1024]{1,0:T(8,128)(2,1)}, u32[]{:S(2)}) copy-start(bf16[1024,1024]{1,0:T(8,128)(2,1)} %param.25) | copy-start | bytes 6291460
  7.2 7.2 copy-start.35
  7.2 44.5 %all-gather.5.cloned.1.call-start = ((), (), s32[]{:S(2)}) async-start(), calls=%async_computation.8 | async-start | bytes 5242880 | tf_op jit(solution)/shard_map/all_gather | solution.py:67
  14.3 166.6 %reduce-scatter.9.cloned.1.call-start = ((), (), s32[]{:S(2)}) async-start(), calls=%async_computation.9 | async-start | bytes 5242880 | tf_op jit(solution)/shard_map/reduce_scatter | solution.py:113
  131.6 49.4 %copy-start.4 = (bf16[1,512,1024]{2,1,0:T(8,128)(2,1)S(1)}, bf16[1,512,1024]{2,1,0:T(8,128)(2,1)}, u32[]{:S(2)}) copy-start(bf16[1,512,1024]{2,1,0:T(8,128)(2,1)} %param.21) | copy-start | bytes 3145732
  131.6 49.4 %copy-start.22 = (f32[1024]{0:T(1024)S(1)}, f32[1024]{0:T(1024)}, u32[]{:S(2)}) copy-start(f32[1024]{0:T(1024)} %param.31) | copy-start | bytes 12292
  136.2 48.3 %copy-start.25 = (f32[1024]{0:T(1024)S(1)}, f32[1024]{0:T(1024)}, u32[]{:S(2)}) copy-start(f32[1024]{0:T(1024)} %param.29) | copy-start | bytes 12292
  136.2 48.3 %copy-start.37 = (f32[1024]{0:T(1024)S(1)}, f32[1024]{0:T(1024)}, u32[]{:S(2)}) copy-start(f32[1024]{0:T(1024)} %param.30) | copy-start | bytes 12292
  136.2 84.5 %all-gather.7.cloned.1.call-start = ((), (), s32[]{:S(2)}) async-start(), calls=%async_computation.10 | async-start | bytes 5242880 | tf_op jit(solution)/shard_map/all_gather | solution.py:119
  186.1 71.2 %all-gather.9.cloned.1.call-start = ((), (), s32[]{:S(2)}) async-start(), calls=%async_computation.12 | async-start | bytes 5242880 | tf_op jit(solution)/shard_map/all_gather | solution.py:133
  188.6 134.2 %reduce-scatter.13.cloned.1.call-start = ((), (), s32[]{:S(2)}) async-start(), calls=%async_computation.13 | async-start | bytes 5242880 | tf_op jit(solution)/shard_map/reduce_scatter | solution.py:139
  278.1 91.6 %reduce-scatter.11.cloned.1.call-start = ((), (), s32[]{:S(2)}) async-start(), calls=%async_computation.11 | async-start | bytes 5242880 | tf_op jit(solution)/shard_map/reduce_scatter | solution.py:125
  290.5 32.3 %copy-start.16 = (bf16[1,512,1024]{2,1,0:T(8,128)(2,1)S(1)}, bf16[1,512,1024]{2,1,0:T(8,128)(2,1)}, u32[]{:S(2)}) copy-start(bf16[1,512,1024]{2,1,0:T(8,128)(2,1)} %reduce-scatter.9.cloned.1.call-done) | copy-start | bytes 3145732
  290.6 79.2 %copy-start.36 = (f32[1024]{0:T(1024)S(1)}, f32[1024]{0:T(1024)}, u32[]{:S(2)}) copy-start(f32[1024]{0:T(1024)} %param.32) | copy-start | bytes 12292
  290.6 120.6 %all-gather.11.cloned.1.call-start = ((), (), s32[]{:S(2)}) async-start(), calls=%async_computation.14 | async-start | bytes 5242880 | tf_op jit(solution)/shard_map/all_gather | solution.py:146
  322.8 47.0 %copy-start.18 = (bf16[1,512,1024]{2,1,0:T(8,128)(2,1)S(1)}, bf16[1,512,1024]{2,1,0:T(8,128)(2,1)}, u32[]{:S(2)}) copy-start(bf16[1,512,1024]{2,1,0:T(8,128)(2,1)} %reduce-scatter.13.cloned.1.call-done) | copy-start | bytes 3145732
  374.0 37.1 %copy-start.40 = (bf16[256,1024]{1,0:T(8,128)(2,1)S(1)}, bf16[256,1024]{1,0:T(8,128)(2,1)}, u32[]{:S(2)}) copy-start(bf16[256,1024]{1,0:T(8,128)(2,1)} %param.24) | copy-start | bytes 1572868
  376.5 39.1 %copy-start.7 = (bf16[1,2048,2,128]{3,1,2,0:T(8,128)(2,1)S(1)}, bf16[1,2048,2,128]{3,1,2,0:T(8,128)(2,1)}, u32[]{:S(2)}) copy-start(bf16[1,2048,2,128]{3,1,2,0:T(8,128)(2,1)} %copy-done.6) | copy-start | bytes 3145732
  376.5 39.1 %copy-start.14 = (bf16[1,2048,2,128]{3,1,2,0:T(8,128)(2,1)S(1)}, bf16[1,2048,2,128]{3,1,2,0:T(8,128)(2,1)}, u32[]{:S(2)}) copy-start(bf16[1,2048,2,128]{3,1,2,0:T(8,128)(2,1)} %get-tuple-element.796) | copy-start | bytes 3145732
  376.5 279.3 %reduce-scatter.17.cloned.1.call-start = ((), (), s32[]{:S(2)}) async-start(), calls=%async_computation.16 | async-start | bytes 3538944 | tf_op jit(solution)/shard_map/reduce_scatter | solution.py:209
  429.7 5.8 copy-start.12
  435.5 13.0 %copy-start.8 = (f32[1,2048,2,128]{1,3,2,0:T(8,128)S(1)}, f32[1,2048,2,128]{1,3,2,0:T(8,128)}, u32[]{:S(2)}) copy-start(f32[1,2048,2,128]{1,3,2,0:T(8,128)} %get-tuple-element.742) | copy-start | bytes 6291460 | tf_op jit(solution)/shard_map/while
  444.1 4.3 copy-start.3
  466.8 5.8 copy-start.12
  472.6 12.9 %copy-start.8 = (f32[1,2048,2,128]{1,3,2,0:T(8,128)S(1)}, f32[1,2048,2,128]{1,3,2,0:T(8,128)}, u32[]{:S(2)}) copy-start(f32[1,2048,2,128]{1,3,2,0:T(8,128)} %get-tuple-element.742) | copy-start | bytes 6291460 | tf_op jit(solution)/shard_map/while
  481.3 4.3 copy-start.3
  503.9 5.8 copy-start.12
  509.7 12.9 %copy-start.8 = (f32[1,2048,2,128]{1,3,2,0:T(8,128)S(1)}, f32[1,2048,2,128]{1,3,2,0:T(8,128)}, u32[]{:S(2)}) copy-start(f32[1,2048,2,128]{1,3,2,0:T(8,128)} %get-tuple-element.742) | copy-start | bytes 6291460 | tf_op jit(solution)/shard_map/while
  518.4 4.3 copy-start.3
  541.0 5.8 copy-start.12
  546.8 12.9 %copy-start.8 = (f32[1,2048,2,128]{1,3,2,0:T(8,128)S(1)}, f32[1,2048,2,128]{1,3,2,0:T(8,128)}, u32[]{:S(2)}) copy-start(f32[1,2048,2,128]{1,3,2,0:T(8,128)} %get-tuple-element.742) | copy-start | bytes 6291460 | tf_op jit(solution)/shard_map/while
  555.4 4.3 copy-start.3
  568.1 4.6 copy-start.19
  572.8 7.8 copy-start.21
  580.5 121.6 %reduce-scatter.15.cloned.1.call-start = ((), (), s32[]{:S(2)}) async-start(), calls=%async_computation.15 | async-start | bytes 5242880 | tf_op jit(solution)/shard_map/reduce_scatter | solution.py:202
  587.0 208.1 %reduce-scatter.21.cloned.1.call-start = ((), (), s32[]{:S(2)}) async-start(), calls=%async_computation.18 | async-start | bytes 4718592 | tf_op jit(solution)/shard_map/reduce_scatter | solution.py:211
  597.3 290.8 %reduce-scatter.23.cloned.1.call-start = ((), (), s32[]{:S(2)}) async-start(), calls=%async_computation.19 | async-start | bytes 4718592 | tf_op jit(solution)/shard_map/reduce_scatter | solution.py:212
  609.8 92.3 %copy-start.5 = (bf16[1,512,1024]{2,1,0:T(8,128)(2,1)S(1)}, bf16[1,512,1024]{2,1,0:T(8,128)(2,1)}, u32[]{:S(2)}) copy-start(bf16[1,512,1024]{2,1,0:T(8,128)(2,1)} %param.21) | copy-start | bytes 3145732
  609.9 92.3 %copy-start.24 = (f32[512]{0:T(512)S(1)}, f32[512]{0:T(512)}, u32[]{:S(2)}) copy-start(f32[512]{0:T(512)} %copy-done.23) | copy-start | bytes 6148
  609.9 92.3 %copy-start.26 = (f32[1024]{0:T(1024)S(1)}, f32[1024]{0:T(1024)}, u32[]{:S(2)}) copy-start(f32[1024]{0:T(1024)} %param.27) | copy-start | bytes 12292
  609.9 94.2 %copy-start.30 = (f32[512]{0:T(512)S(1)}, f32[512]{0:T(512)}, u32[]{:S(2)}) copy-start(f32[512]{0:T(512)} %copy-done.29) | copy-start | bytes 6148
  609.9 94.2 %copy-start.28 = (f32[512]{0:T(512)S(1)}, f32[512]{0:T(512)}, u32[]{:S(2)}) copy-start(f32[512]{0:T(512)} %copy-done.27) | copy-start | bytes 6148
  609.9 345.8 %reduce-scatter.19.cloned.1.call-start = ((), (), s32[]{:S(2)}) async-start(), calls=%async_computation.17 | async-start | bytes 1179648 | tf_op jit(solution)/shard_map/reduce_scatter | solution.py:210
  615.6 91.1 %copy-start.31 = (f32[1024]{0:T(1024)S(1)}, f32[1024]{0:T(1024)}, u32[]{:S(2)}) copy-start(f32[1024]{0:T(1024)} %get-tuple-element.528) | copy-start | bytes 12292
  615.6 91.1 %copy-start.32 = (f32[1024]{0:T(1024)S(1)}, f32[1024]{0:T(1024)}, u32[]{:S(2)}) copy-start(f32[1024]{0:T(1024)} %get-tuple-element.538) | copy-start | bytes 12292
  615.6 91.1 %copy-start.33 = (f32[1024]{0:T(1024)S(1)}, f32[1024]{0:T(1024)}, u32[]{:S(2)}) copy-start(f32[1024]{0:T(1024)} %get-tuple-element.476) | copy-start | bytes 12292
  615.6 91.1 %copy-start.34 = (f32[1024]{0:T(1024)S(1)}, f32[1024]{0:T(1024)}, u32[]{:S(2)}) copy-start(f32[1024]{0:T(1024)} %get-tuple-element.472) | copy-start | bytes 12292
  704.0 251.6 %copy-start.1 = (bf16[1024,1024]{1,0:T(8,128)(2,1)S(1)}, bf16[1024,1024]{1,0:T(8,128)(2,1)}, u32[]{:S(2)}) copy-start(bf16[1024,1024]{1,0:T(8,128)(2,1)} %param.25) | copy-start | bytes 6291460
  (27 other events, 69.1 us)
Sparse Core Ops, SparseCore 0:
  14.5 37.1 all-gather.4
  136.4 44.5 reduce-scatter.8
  186.2 34.4 all-gather.6
  222.8 34.4 all-gather.8
  278.2 44.5 reduce-scatter.12
  325.2 44.5 reduce-scatter.10
  376.6 34.4 all-gather.10
  580.6 75.1 reduce-scatter.16
  658.5 43.5 reduce-scatter.14
  706.2 88.9 reduce-scatter.20
  799.8 88.2 reduce-scatter.22
  891.9 63.6 reduce-scatter.18
where the time goes:
time: 974 us; the launch traced here: 963 us
  waiting for transfers between devices  527 us (54%)
  matrix products  207 us (21%)
  other arithmetic  97.9 us (10%)
  blocking collectives  48.2 us (5%)
  local copies, waits for them, and re-layouts  42 us (4%)
  loops' own time  24.2 us (2%)
  between operations  15 us (2%)
    reduce_scatter x1, waiting for transfers between devices, local(): lax.psum_scatter(down_grad, 'dp', scatter_dimension=1, tiled=True)  92.9 us
    reduce_scatter x1, waiting for transfers between devices, local(): lax.psum_scatter(out_grad, 'dp', scatter_dimension=1, tiled=True)  67.6 us
    reduce_scatter x1, waiting for transfers between devices, local(): lax.psum_scatter(attn_part.astype(jnp.bfloat16), 'tensor', scatter_dimens...  44.4 us
    reduce_scatter x1, waiting for transfers between devices, local(): lax.psum_scatter(grad_inputs.astype(jnp.bfloat16), 'tensor', scatter_dime...  44.4 us
    unnamed x1, blocking collectives  42 us
    reduce_scatter x1, waiting for transfers between devices, local(): lax.psum_scatter(ffn_part.astype(jnp.bfloat16), 'tensor', scatter_dimensi...  41 us
    reduce_scatter x1, waiting for transfers between devices, local(): lax.psum_scatter(qkv_grad, 'dp', scatter_dimension=1, tiled=True)  40.2 us
    reduce_scatter x1, waiting for transfers between devices, local(): lax.psum_scatter(up_grad, 'dp', scatter_dimension=0, tiled=True)  39 us
  transfers between devices with their start and end apart: 12, of which 12 were waited for; matrix products, arithmetic and copies ran while one was open for 8% of the time, Pallas kernels for 0%

commit v1 on v0

v1 whole, which is shorter than its diff:
```python
import functools

import jax
import jax.numpy as jnp
from jax import lax
from jax.experimental import pallas as pl
from jax.experimental.pallas import tpu as pltpu
from jax.sharding import PartitionSpec as P

H = 8
HD = 128
EPS = 1e-05
NEG = -1e30
LOG2E = 1.4426950408889634
BF = jnp.bfloat16
F32 = jnp.float32
NN = (((1,), (0,)), ((), ()))
NT = (((1,), (1,)), ((), ()))
TN = (((0,), (0,)), ((), ()))
VMEM = pl.BlockSpec(memory_space=pltpu.VMEM)
SMEM = pl.BlockSpec(memory_space=pltpu.SMEM)


def dot(a, b, dims=NN):
    return lax.dot_general(a, b, dims, preferred_element_type=F32)


def split3(v):
    hi = v.astype(BF)
    rest = v - hi.astype(F32)
    mid = rest.astype(BF)
    return hi, mid, (rest - mid.astype(F32)).astype(BF)


def attn_fwd_kernel(size, block, heads, t_ref, qkv_ref, qx_ref, kx_ref, o_ref, qx2_ref, qa, ka, va):
    t = t_ref[0]
    pieces = 4
    width = heads * HD
    lane = lax.broadcasted_iota(jnp.int32, (size, HD), 1)
    ones = jnp.where(lane == 0, 1.0, 0.0).astype(BF)
    for r in range(pieces):
        to = pl.ds(pl.multiple_of((t ^ r) * size, size), size)
        src = slice(r * size, (r + 1) * size)
        for h in range(heads):
            qa[h, to, :HD] = qkv_ref[src, h * HD : (h + 1) * HD]
            ka[h, to, :HD] = qkv_ref[src, width + h * HD : width + (h + 1) * HD]
            va[h, to, :HD] = qkv_ref[src, 2 * width + h * HD : 2 * width + (h + 1) * HD]
            va[h, to, HD:] = ones
            qa[h, to, HD:] = qx_ref[src, :]
            ka[h, to, HD:] = kx_ref[h, src, :]
    row = lax.broadcasted_iota(jnp.int32, (block, block), 0)
    col = lax.broadcasted_iota(jnp.int32, (block, block), 1)
    keep = col <= row
    lane = lax.broadcasted_iota(jnp.int32, (block, HD), 1)
    per = size // block
    for i in range(pieces * per):
        start = i * block
        end = start + block
        at = pl.ds(pl.multiple_of(((i // per) ^ t) * size + (i % per) * block, block), block)
        for h in range(heads):
            q = qa[h, start:end, :]
            near = jnp.where(keep, dot(q, ka[h, start:end, :], NT), NEG)
            top = jnp.max(near, -1, keepdims=True)
            if i:
                far = dot(q, ka[h, :start, :], NT)
                top = jnp.maximum(top, jnp.max(far, -1, keepdims=True))
            out = dot(jnp.exp2(near - top).astype(BF), va[h, start:end, :])
            if i:
                out = out + dot(jnp.exp2(far - top).astype(BF), va[h, :start, :])
            total = out[:, HD : HD + 1]
            o_ref[at, h * HD : (h + 1) * HD] = (out[:, :HD] / total).astype(BF)
            hi, mid, lo = split3(-(top + jnp.log2(total)))
            extra = qa[h, start:end, HD:]
            extra = jnp.where(lane == 7, hi, jnp.where(lane == 8, mid, jnp.where(lane == 9, lo, extra)))
            qx2_ref[h, at, :] = extra


def attn_fwd(t, qkv, qx, kx, block=512):
    length = qkv.shape[0]
    width = qkv.shape[1] // 3
    heads = width // HD
    return pl.pallas_call(
        functools.partial(attn_fwd_kernel, length // 4, block, heads),
        out_shape=(
            jax.ShapeDtypeStruct((length, width), BF),
            jax.ShapeDtypeStruct((heads, length, HD), BF),
        ),
        in_specs=[SMEM, VMEM, VMEM, VMEM],
        out_specs=(VMEM, VMEM),
        scratch_shapes=[pltpu.VMEM((heads, length, 2 * HD), BF)] * 3,
        name="attn_fwd",
        cost_estimate=pl.CostEstimate(flops=8 * 10**9, bytes_accessed=16 * 10**6, transcendentals=0),
        compiler_params=pltpu.CompilerParams(vmem_limit_bytes=56 * 2**20),
    )(t, qkv, qx, kx)


def attn_bwd_kernel(size, block, heads, t_ref, qkv_ref, do_ref, o_ref, qx_ref, kx_ref, g_ref, qa, ka, da, va, dqt):
    t = t_ref[0]
    pieces = 4
    length = pieces * size
    width = heads * HD
    lane = lax.broadcasted_iota(jnp.int32, (size, HD), 1)
    ones = jnp.where(lane < 3, 1.0, 0.0).astype(BF)
    for r in range(pieces):
        to = pl.ds(pl.multiple_of((t ^ r) * size, size), size)
        src = slice(r * size, (r + 1) * size)
        for h in range(heads):
            sl = slice(h * HD, (h + 1) * HD)
            qa[h, to, :HD] = qkv_ref[src, sl]
            qa[h, to, HD:] = qx_ref[h, src, :]
            ka[h, to, :HD] = qkv_ref[src, width + h * HD : width + (h + 1) * HD]
            ka[h, to, HD:] = kx_ref[h, src, :]
            va[h, to, :HD] = qkv_ref[src, 2 * width + h * HD : 2 * width + (h + 1) * HD]
            va[h, to, HD:] = ones
            do = do_ref[src, sl]
            delta = jnp.sum(do.astype(F32) * o_ref[src, sl].astype(F32), -1, keepdims=True)
            hi, mid, lo = split3(-delta)
            da[h, to, :HD] = do
            da[h, to, HD:] = jnp.where(lane == 0, hi, jnp.where(lane == 1, mid, jnp.where(lane == 2, lo, BF(0))))
    row = lax.broadcasted_iota(jnp.int32, (block, block), 0)
    col = lax.broadcasted_iota(jnp.int32, (block, block), 1)
    keep = row <= col
    per = size // block
    for j in range(pieces * per):
        start = j * block
        end = start + block
        at = pl.ds(pl.multiple_of(((j // per) ^ t) * size + (j % per) * block, block), block)
        for h in range(heads):
            k = ka[h, start:end, :]
            v = va[h, start:end, :]

            def part(a, b, masked):
                s = dot(k, qa[h, a:b, :], NT)
                if masked:
                    s = jnp.where(keep, s, NEG)
                p = jnp.exp2(s)
                ds = (p * dot(v, da[h, a:b, :], NT)).astype(BF)
                dv = dot(p.astype(BF), da[h, a:b, :HD])
                dk = dot(ds, qa[h, a:b, :HD])
                dq = dot(k[:, :HD], ds, TN)
                if j:
                    dqt[h, :, a:b] += dq
                else:
                    dqt[h, :, a:b] = dq
                return dk, dv

            dk, dv = part(start, end, True)
            if end < length:
                dk_far, dv_far = part(end, length, False)
                dk, dv = dk + dk_far, dv + dv_far
            g_ref[at, h * HD : (h + 1) * HD] = (dqt[h, :, start:end].T * HD**-0.5).astype(BF)
            g_ref[at, width + h * HD : width + (h + 1) * HD] = (dk * (1.0 / LOG2E)).astype(BF)
            g_ref[at, 2 * width + h * HD : 2 * width + (h + 1) * HD] = dv.astype(BF)


def attn_bwd(t, qkv, do, o, qx, kx, block=512):
    length = qkv.shape[0]
    width = qkv.shape[1] // 3
    heads = width // HD
    return pl.pallas_call(
        functools.partial(attn_bwd_kernel, length // 4, block, heads),
        out_shape=jax.ShapeDtypeStruct(qkv.shape, BF),
        in_specs=[SMEM] + [VMEM] * 5,
        out_specs=VMEM,
        scratch_shapes=[pltpu.VMEM((heads, length, 2 * HD), BF)] * 4 + [pltpu.VMEM((heads, HD, length), F32)],
        name="attn_bwd",
        cost_estimate=pl.CostEstimate(flops=14 * 10**9, bytes_accessed=24 * 10**6, transcendentals=0),
        compiler_params=pltpu.CompilerParams(vmem_limit_bytes=56 * 2**20),
    )(t, qkv, do, o, qx, kx)


def position_columns(t, segments, heads):
    length = segments.shape[0]
    size = length // 4
    lane = jnp.arange(HD, dtype=jnp.int32)[None, :]
    hot = (segments[:, None] == lane - 3) & (lane >= 3) & (lane < 7)
    qx = jnp.where((lane < 3) | hot, 1.0, 0.0).astype(BF)
    index = jnp.arange(length, dtype=jnp.int32)
    place = ((index // size) ^ t) * size + index % size
    slopes = jnp.exp2(-8.0 * (t * heads + 1 + jnp.arange(heads, dtype=jnp.int32)).astype(F32) / H) * LOG2E
    bias = slopes[:, None, None] * place.astype(F32)[None, :, None]
    hi = lax.reduce_precision(bias, 8, 7)
    mid = lax.reduce_precision(bias - hi, 8, 7)
    lo = bias - hi - mid
    base = jnp.where(
        (lane >= 3) & (lane < 7), jnp.where(hot, 0.0, NEG), jnp.where((lane >= 7) & (lane < 10), 1.0, 0.0)
    )[None]
    kx = jnp.where(lane == 0, hi, jnp.where(lane == 1, mid, jnp.where(lane == 2, lo, base))).astype(BF)
    return qx, kx


def to_core(x):
    return lax.ppermute(x, "tensor", [(i, i ^ 1) for i in range(4)])


def to_chip(x):
    return lax.ppermute(x, "tensor", [(i, i ^ 2) for i in range(4)])


def to_diag(x):
    return lax.ppermute(x, "tensor", [(i, i ^ 3) for i in range(4)])


def gather(x):
    far = to_chip(x)
    return [x, to_core(x), far, to_core(far)]


def scatter_sum(parts):
    chip = (parts[2].astype(F32) + to_core(parts[3]).astype(F32)).astype(BF)
    return parts[0].astype(F32) + to_core(parts[1]).astype(F32) + to_chip(chip).astype(F32)


def dp_steps(size, first):
    bits = list(range(size.bit_length() - 1))
    return bits[first:] + bits[:first]


def dp_reduce(x, size, index, first):
    bits = size.bit_length() - 1
    shape = x.shape[1:]
    x = x.reshape((2,) * bits + shape)
    axes = list(range(bits - 1, -1, -1))
    for bit in dp_steps(size, first):
        axis = axes.index(bit)
        mine = (index >> bit) & 1
        send = lax.dynamic_index_in_dim(x, 1 - mine, axis, keepdims=False).astype(BF)
        keep = lax.dynamic_index_in_dim(x, mine, axis, keepdims=False)
        got = lax.ppermute(send, "dp", [(i, i ^ (1 << bit)) for i in range(size)])
        x = keep.astype(F32) + got.astype(F32)
        axes.remove(bit)
    return x


def layer_norm(values, gain, shift):
    center = values - jnp.mean(values, -1, keepdims=True)
    spread = jnp.mean(center * center, -1, keepdims=True)
    return center * lax.rsqrt(spread + EPS) * gain + shift


def normalized(values):
    center = values - jnp.mean(values, -1, keepdims=True)
    inverse = lax.rsqrt(jnp.mean(center * center, -1, keepdims=True) + EPS)
    return center * inverse, inverse


def norm_back(grad, gain, hat, inverse):
    e = grad * gain
    return (e - jnp.mean(e, -1, keepdims=True) - hat * jnp.mean(e * hat, -1, keepdims=True)) * inverse


def gelu_smooth(values):
    return jax.nn.gelu(values, approximate=True)


def local(dp, block_input, segment_ids, w_qkv, w_out, w_up, w_down, ln1_gain, ln1_bias, ln2_gain, ln2_bias, out_bias, down_bias, cotangent):
    size, width = block_input.shape[1:]
    length = 4 * size
    local_width = w_qkv.shape[2]
    heads = local_width // HD
    t = lax.axis_index("tensor")
    d = lax.axis_index("dp")
    t_arg = t[None].astype(jnp.int32)
    x = block_input[0].astype(F32)
    seg = segment_ids[0]
    hat_one, inverse_one = normalized(x)
    n1 = (hat_one * ln1_gain + ln1_bias).astype(BF)
    segments = jnp.concatenate(gather(seg))
    qx, kx = position_columns(t, segments, heads)
    n1_all = jnp.concatenate(gather(n1))
    valid = (seg != 0).astype(F32)[:, None]
    grad_out = valid * cotangent[0].astype(F32)
    dffn_own = grad_out.astype(BF)
    wo = gather(w_out)
    dffn = jnp.concatenate(gather(dffn_own))

    q_scale = HD**-0.5 * LOG2E
    projected = [dot(n1_all, w_qkv[c]) for c in range(3)]
    qkv = jnp.concatenate([projected[0] * q_scale, projected[1], projected[2]], -1).astype(BF)
    mixed, qx2 = attn_fwd(t_arg, qkv, qx, kx)
    mixed_sent = mixed.reshape(4, size, local_width)
    mixed_own = jnp.concatenate(
        [mixed_sent[0], to_core(mixed_sent[1]), to_chip(mixed_sent[2]), to_diag(mixed_sent[3])], -1
    )
    wo_all = jnp.concatenate(wo)
    resid = x + dot(mixed_own, wo_all) + out_bias
    hat_two, inverse_two = normalized(resid)
    n2 = jnp.concatenate(gather((hat_two * ln2_gain + ln2_bias).astype(BF)))
    pre = dot(n2, w_up)
    activated, gelu_back = jax.vjp(gelu_smooth, pre)
    act = activated.astype(BF)
    dact = dot(dffn, w_down, NT)
    dpre = gelu_back(dact)[0].astype(BF)
    dn2_parts = dot(dpre, w_up, NT).astype(BF).reshape(4, size, width)
    dn2 = scatter_sum(dn2_parts)
    ffn_parts = dot(act, w_down).astype(BF).reshape(4, size, width)
    up_grad = dot(n2, dpre, TN)
    down_grad = dot(act, dffn, TN)

    dresid = grad_out + norm_back(dn2, ln2_gain, hat_two, inverse_two)
    dattn = dresid.astype(BF)
    dmixed_own = dot(dattn, wo_all, NT).astype(BF).reshape(size, 4, local_width)
    dmixed = jnp.concatenate(
        [dmixed_own[:, 0], to_core(dmixed_own[:, 1]), to_chip(dmixed_own[:, 2]), to_diag(dmixed_own[:, 3])]
    )
    out_grad = dot(mixed_own, dattn, TN).astype(BF).reshape(4, local_width, width)
    ffn = scatter_sum(ffn_parts)
    output = (valid * (resid + ffn + down_bias)).astype(BF)
    dqkv = attn_bwd(t_arg, qkv, dmixed, mixed, qx2, kx)
    w_flat = jnp.concatenate([w_qkv[0], w_qkv[1], w_qkv[2]], -1)
    dn1 = scatter_sum(dot(dqkv, w_flat, NT).astype(BF).reshape(4, size, width))
    qkv_grad = dot(n1_all, dqkv, TN)
    x_grad = dresid + norm_back(dn1, ln1_gain, hat_one, inverse_one)

    out_sum = scatter_sum(out_grad)
    up_rows = width // dp
    qkv_sum = dp_reduce(qkv_grad.reshape(dp, up_rows, 3 * local_width), dp, d, 0)
    qkv_final = qkv_sum.reshape(up_rows, 3, local_width).transpose(1, 0, 2)
    up_final = dp_reduce(up_grad.reshape(dp, up_rows, w_up.shape[1]), dp, d, 0)
    down_final = dp_reduce(down_grad.reshape(w_down.shape[0], dp, up_rows).transpose(1, 0, 2), dp, d, 1)
    out_final = dp_reduce(out_sum.reshape(local_width, dp, up_rows).transpose(1, 0, 2), dp, d, 1)
    vectors = jnp.stack(
        [
            jnp.sum(dn1 * hat_one, 0),
            jnp.sum(dn1, 0),
            jnp.sum(dn2 * hat_two, 0),
            jnp.sum(dn2, 0),
            jnp.sum(dresid, 0),
            jnp.sum(grad_out, 0),
        ]
    )
    bits = dp.bit_length() - 1
    chunk = width // dp // 4
    vectors = vectors.reshape(6, dp, 4, chunk).transpose(1, 2, 0, 3)
    for step in range(2):
        bit = 1 - step
        mine = (t >> bit) & 1
        view = vectors.reshape((dp,) + (2,) * (2 - step) + (6, chunk))
        send = lax.dynamic_index_in_dim(view, 1 - mine, 1, keepdims=False)
        vectors = lax.dynamic_index_in_dim(view, mine, 1, keepdims=False) + lax.ppermute(
            send, "tensor", [(i, i ^ (1 << bit)) for i in range(4)]
        )
    vectors = vectors.reshape((2,) * bits + (6, chunk))
    for bit in range(bits - 1, -1, -1):
        mine = (d >> bit) & 1
        send = lax.dynamic_index_in_dim(vectors, 1 - mine, 0, keepdims=False)
        vectors = lax.dynamic_index_in_dim(vectors, mine, 0, keepdims=False) + lax.ppermute(
            send, "dp", [(i, i ^ (1 << bit)) for i in range(dp)]
        )
    return (
        output[None],
        x_grad[None],
        qkv_final,
        out_final.reshape(local_width, up_rows),
        up_final,
        down_final.reshape(w_down.shape[0], up_rows),
        vectors[0],
        vectors[1],
        vectors[2],
        vectors[3],
        vectors[4],
        vectors[5],
    )


def solution(mesh):
    row = P("dp", "tensor", None)
    in_specs = (
        row,
        P("dp", "tensor"),
        P(None, None, "tensor"),
        P("tensor", None),
        P(None, "tensor"),
        P("tensor", None),
        P(),
        P(),
        P(),
        P(),
        P(),
        P(),
        row,
    )
    vector = P(("dp", "tensor"))
    out_specs = (row, row, P(None, "dp", "tensor"), P("tensor", "dp"), P("dp", "tensor"), P("tensor", "dp")) + (vector,) * 6
    run = functools.partial(local, mesh.shape["dp"])
    return jax.shard_map(run, mesh=mesh, in_specs=in_specs, out_specs=out_specs, check_vma=False)
```

time: 974 us -> 428 us (0.44)
  waiting for transfers between devices: 527 us -> 191 us
  matrix products: 207 us -> 74.6 us
  other arithmetic: 97.9 us -> 39.8 us
  blocking collectives: 48.2 us -> 0 us
  starting transfers between devices: 1.54 us -> 39.1 us
  Pallas kernels: 0 us -> 32.4 us
  loops' own time: 24.2 us -> 0 us
  between operations: 15 us -> 1.97 us
    reduce_scatter x8 -> x0, waiting for transfers between devices: 402 us -> none  [the longest x1 92.9 us: local(): lax.psum_scatter(down_grad, 'dp', scatter_dimension=1, tiled=True)]
    ppermute x0 -> x50, waiting for transfers between devices: none -> 191 us  [the longest x11 113 us: to_chip(): return lax.ppermute(x, 'tensor', [(i, i ^ 2) for i in range(4)])]
    dot_general x40 -> x14, matrix products: 207 us -> 74.6 us  [dot(): return lax.dot_general(a, b, dims, preferred_element_type=F32)]
    all_gather x4 -> x0, waiting for transfers between devices: 125 us -> none  [the longest x1 34.4 us: local(): lax.all_gather(grad_resid.astype(jnp.bfloat16), 'tensor', axis=1, tiled=T...]
    unnamed x1 -> x0, blocking collectives: 42 us -> none
    ppermute x0 -> x50, starting transfers between devices: none -> 39.1 us  [the longest x11 16.1 us: to_chip(): return lax.ppermute(x, 'tensor', [(i, i ^ 2) for i in range(4)])]
    pallas_call x0 -> x2, Pallas kernels: none -> 32.4 us  [the longest x1 20.5 us: attn_bwd(): pl.pallas_call(functools.partial(attn_bwd_kernel, length // 4, block, hea...]
    convert_element_type x18 -> x11, other arithmetic: 45 us -> 13 us  [the longest x4 4.73 us: scatter_sum(): chip = (parts[2].astype(F32) + to_core(parts[3]).astype(F32)).astype(BF)]
  transfers between devices with their start and end apart: 12 -> 50, of which waited for: 12 -> 24; matrix products, arithmetic and copies ran while one was open for 8% -> 27% of each run, Pallas kernels for 0% -> 8%
where the time goes in v1:
time: 428 us; the launch traced here: 422 us
  waiting for transfers between devices  191 us (45%)
  matrix products  74.6 us (17%)
  local copies, waits for them, and re-layouts  43.2 us (10%)
  other arithmetic  39.8 us (9%)
  starting transfers between devices  39.1 us (9%)
  Pallas kernels  32.4 us (8%)
    ppermute x11, waiting for transfers between devices, to_chip(): return lax.ppermute(x, 'tensor', [(i, i ^ 2) for i in range(4)])  113 us
    dot_general x14, matrix products, dot(): return lax.dot_general(a, b, dims, preferred_element_type=F32)  74.6 us
    ppermute x12, waiting for transfers between devices, dp_reduce(): got = lax.ppermute(send, 'dp', [(i, i ^ 1 << bit) for i in range(size)])  63.6 us
    pallas_call x1, Pallas kernels, attn_bwd(): pl.pallas_call(functools.partial(attn_bwd_kernel, length // 4, block, hea...  20.5 us
    unnamed x114, local copies, waits for them, and re-layouts  20 us
    ppermute x11, starting transfers between devices, to_chip(): return lax.ppermute(x, 'tensor', [(i, i ^ 2) for i in range(4)])  16.1 us
    ppermute x12, starting transfers between devices, dp_reduce(): got = lax.ppermute(send, 'dp', [(i, i ^ 1 << bit) for i in range(size)])  14.1 us
    pallas_call x1, Pallas kernels, attn_fwd(): pl.pallas_call(functools.partial(attn_fwd_kernel, length // 4, block, hea...  11.9 us
  transfers between devices with their start and end apart: 50, of which 24 were waited for; matrix products, arithmetic and copies ran while one was open for 27% of the time, Pallas kernels for 8%

profile of v1, /device:TPU:0, one launch (start us, length us, event | category | flops | bytes accessed | tf_op | source)
XLA Modules:
  0.0 422.3 jit_solution(2597528190257385844)
XLA Ops:
  0.7 3.0 collective-permute-start.4
  9.1 2.0 collective-permute-start.1
  13.8 27.1 %collective-permute-done.1 = bf16[512,1024]{1,0:T(8,128)(2,1)} collective-permute-done((bf16[512,1024]{1,0:T(8,128)(2,1)S(1)}, bf16[512,1024]{1,0:T(8,128)(2,1)}, u32[]{:S(2)}, u32[]{:S(2)}) %collective-permute-start.1) | collective-permute-done | bytes 1048608 | tf_op jit(solution)/shard_map/ppermute | solution.py:197
  42.3 2.9 select_convert_fusion.kx_ref
  45.7 3.2 convolution_convert_fusion.4
  49.0 2.5 convolution_convert_fusion.3
  51.5 2.5 fusion.9
  54.0 2.0 pad_maximum_fusion.3.qkv_ref
  56.0 11.9 %attn_fwd.1 = (bf16[2048,256]{1,0:T(8,128)(2,1)}, bf16[2,2048,128]{2,1,0:T(8,128)(2,1)}) custom-call(s32[1]{0:T(128)} %bitcast.2.t_ref, bf16[2048,768]{1,0:T(8,128)(2,1)} %pad_maximum_fusion.3.qkv_ref, bf16[2048,128]{1,0:T(8,128)(2,1)} %select_convert_fusion.1.qx_ref, bf16[2,2048,128]{2,1,0:T(8,128)(2,1)} %select_convert_fusion.kx_ref), custom_call_target="tpu_custom_call" | custom-call | flops 8000000000 | bytes 16000000 | tf_op jit(solution)/shard_map/attn_fwd/pallas_call | solution.py:82
  73.3 4.3 %collective-permute-done.8 = bf16[512,256]{1,0:T(8,128)(2,1)S(1)} collective-permute-done((bf16[512,256]{1,0:T(8,128)(2,1)S(1)}, bf16[512,256]{1,0:T(8,128)(2,1)S(1)}, u32[]{:S(2)}, u32[]{:S(2)}) %collective-permute-start.8) | collective-permute-done | bytes 262176 | tf_op jit(solution)/shard_map/ppermute | solution.py:201
  77.7 5.8 %collective-permute-done.7 = bf16[512,256]{1,0:T(8,128)(2,1)S(1)} collective-permute-done((bf16[512,256]{1,0:T(8,128)(2,1)S(1)}, bf16[512,256]{1,0:T(8,128)(2,1)S(1)}, u32[]{:S(2)}, u32[]{:S(2)}) %collective-permute-start.7) | collective-permute-done | bytes 262176 | tf_op jit(solution)/shard_map/ppermute | solution.py:197
  90.0 23.1 %collective-permute-done.13 = bf16[512,1024]{1,0:T(8,128)(2,1)} collective-permute-done((bf16[512,1024]{1,0:T(8,128)(2,1)}, bf16[512,1024]{1,0:T(8,128)(2,1)}, u32[]{:S(2)}, u32[]{:S(2)}) %collective-permute-start.13) | collective-permute-done | bytes 1048608 | tf_op jit(solution)/shard_map/ppermute | solution.py:197
  113.6 2.7 slice_bitcast_fusion.2
  116.3 18.2 %collective-permute-done.19 = bf16[512,1024]{1,0:T(8,128)(2,1)} collective-permute-done((bf16[512,1024]{1,0:T(8,128)(2,1)}, bf16[512,1024]{1,0:T(8,128)(2,1)}, u32[]{:S(2)}, u32[]{:S(2)}) %collective-permute-start.19) | collective-permute-done | bytes 1048608 | tf_op jit(solution)/shard_map/ppermute | solution.py:197
  134.6 7.9 %fusion.40 = f32[2048,1024]{1,0:T(8,128)S(1)} fusion(bf16[1024,1024]{1,0:T(8,128)(2,1)S(1)} %copy-done.37, bf16[512,1024]{1,0:T(8,128)(2,1)} %collective-permute-done.14, bf16[512,1024]{1,0:T(8,128)(2,1)} %collective-permute-done.13, bf16[512,1024]{1,0:T(8,128)(2,1)} %collective-permute-done.12, bf16[512,1024]{1,0:T(8,128)(2,1)} %add_convert_fusion.3), kind=kOutput, calls=%fused_computation.91 | convolution fusion | flops 4311744512 | bytes 14680064 | tf_op jit(solution)/shard_map/dot_general | solution.py:25
  142.5 6.8 %convolution_convert_fusion.2 = bf16[2048,1024]{1,0:T(8,128)(2,1)} fusion(bf16[1024,1024]{1,0:T(8,128)(2,1)S(1)} %copy-done, f32[2048,1024]{1,0:T(8,128)S(1)} %fusion.40), kind=kOutput, calls=%fused_computation.15 | convolution fusion | flops 4315938816 | bytes 14680064 | tf_op jit(solution)/shard_map/dot_general | solution.py:25
  149.3 9.1 %fusion.37 = f32[1024,1024]{0,1:T(8,128)} fusion(bf16[512,1024]{1,0:T(8,128)(2,1)S(1)} %collective-permute-done.20, bf16[512,1024]{1,0:T(8,128)(2,1)} %collective-permute-done.19, bf16[512,1024]{1,0:T(8,128)(2,1)} %collective-permute-done.18, bf16[512,1024]{1,0:T(8,128)(2,1)} %fusion.28, f32[2048,1024]{1,0:T(8,128)S(1)} %fusion.40), kind=kOutput, calls=%fused_computation.88 | convolution fusion | flops 4330618880 | bytes 16777216 | tf_op jit(solution)/shard_map/dot_general | solution.py:25
  158.5 5.3 %copy.90 = f32[1024,8,128]{2,0,1:T(8,128)} copy(f32[1024,8,128]{0,2,1:T(8,128)} %bitcast.181) | data formatting | bytes 8388608 | tf_op jit(solution)/shard_map/reshape | solution.py:320
  167.2 13.5 %fusion.6 = bf16[2048,1024]{1,0:T(8,128)(2,1)S(1)} fusion(f32[2048,1024]{1,0:T(8,128)} %copy-done.48, bf16[1024,1024]{1,0:T(8,128)(2,1)S(1)} %copy-done, bf16[512,1024]{1,0:T(8,128)(2,1)} %copy-done.43, bf16[512,1024]{1,0:T(8,128)(2,1)} %collective-permute-done.19, bf16[512,1024]{1,0:T(8,128)(2,1)} %collective-permute-done.18, bf16[512,1024]{1,0:T(8,128)(2,1)} %fusion.28), kind=kOutput, calls=%fused_computation.8 | convolution fusion | flops 4353687552 | bytes 18874368 | tf_op jit(solution)/shard_map/dot_general | solution.py:25
  180.6 6.4 %fusion.39 = f32[1024,1024]{1,0:T(8,128)S(1)} fusion(bf16[2048,1024]{1,0:T(8,128)(2,1)S(1)} %fusion.6, bf16[512,1024]{1,0:T(8,128)(2,1)} %collective-permute-done.14, bf16[512,1024]{1,0:T(8,128)(2,1)} %collective-permute-done.13, bf16[512,1024]{1,0:T(8,128)(2,1)} %collective-permute-done.12, bf16[512,1024]{1,0:T(8,128)(2,1)} %add_convert_fusion.3), kind=kOutput, calls=%fused_computation.90 | convolution fusion | flops 4311744512 | bytes 12582912 | tf_op jit(solution)/shard_map/dot_general | solution.py:25
  188.8 5.0 %convolution_convert_fusion.1 = bf16[2048,1024]{1,0:T(8,128)(2,1)S(1)} fusion(bf16[2048,1024]{1,0:T(8,128)(2,1)S(1)} %fusion.6, bf16[1024,1024]{1,0:T(8,128)(2,1)S(1)} %copy-done.38), kind=kOutput, calls=%fused_computation.14 | convolution fusion | flops 4297064448 | bytes 10485760 | tf_op jit(solution)/shard_map/dot_general | solution.py:25
  194.0 1.9 copy-done.14
  197.5 15.0 %collective-permute-done.39 = bf16[2,2,128,1024]{3,2,0,1:T(8,128)(2,1)S(1)} collective-permute-done((bf16[2,2,128,1024]{3,2,0,1:T(8,128)(2,1)S(1)}, bf16[2,2,128,1024]{3,2,0,1:T(8,128)(2,1)S(1)}, u32[]{:S(2)}, u32[]{:S(2)}) %collective-permute-start.39) | collective-permute-done | bytes 1048608 | tf_op jit(solution)/shard_map/ppermute | solution.py:229
  212.6 2.6 collective-permute-start.43
  216.6 21.3 %collective-permute-done.43 = bf16[2,1024,128]{2,1,0:T(8,128)(2,1)S(1)} collective-permute-done((bf16[2,1024,128]{2,1,0:T(8,128)(2,1)S(1)}, bf16[2,1024,128]{2,1,0:T(8,128)(2,1)S(1)}, u32[]{:S(2)}, u32[]{:S(2)}) %collective-permute-start.43) | collective-permute-done | bytes 524320 | tf_op jit(solution)/shard_map/ppermute | solution.py:229
  242.0 4.5 %collective-permute-done.44 = bf16[1024,128]{1,0:T(8,128)(2,1)S(1)} collective-permute-done((bf16[1024,128]{1,0:T(8,128)(2,1)S(1)}, bf16[1024,128]{1,0:T(8,128)(2,1)S(1)}, u32[]{:S(2)}, u32[]{:S(2)}) %collective-permute-start.44) | collective-permute-done | bytes 262176 | tf_op jit(solution)/shard_map/ppermute | solution.py:229
  248.9 4.9 %collective-permute-done.41 = bf16[128,1024]{1,0:T(8,128)(2,1)S(1)} collective-permute-done((bf16[128,1024]{1,0:T(8,128)(2,1)S(1)}, bf16[128,1024]{1,0:T(8,128)(2,1)S(1)}, u32[]{:S(2)}, u32[]{:S(2)}) %collective-permute-start.41) | collective-permute-done | bytes 262176 | tf_op jit(solution)/shard_map/ppermute | solution.py:229
  254.7 9.3 %collective-permute-done.23 = bf16[512,1024]{1,0:T(8,128)(2,1)S(1)} collective-permute-done((bf16[512,1024]{1,0:T(8,128)(2,1)S(1)}, bf16[512,1024]{1,0:T(8,128)(2,1)S(1)}, u32[]{:S(2)}, u32[]{:S(2)}) %collective-permute-start.23) | collective-permute-done | bytes 1048608 | tf_op jit(solution)/shard_map/ppermute | solution.py:197
  265.2 20.2 %collective-permute-done.17 = bf16[512,1024]{1,0:T(8,128)(2,1)S(1)} collective-permute-done((bf16[512,1024]{1,0:T(8,128)(2,1)S(1)}, bf16[512,1024]{1,0:T(8,128)(2,1)S(1)}, u32[]{:S(2)}, u32[]{:S(2)}) %collective-permute-start.17) | collective-permute-done | bytes 1048608 | tf_op jit(solution)/shard_map/ppermute | solution.py:197
  285.4 2.9 fusion.80
  289.6 2.4 convolution_convert_fusion.6
  292.0 2.0 copy.80
  300.9 2.5 convolution_convert_fusion.5
  307.3 4.2 %collective-permute-done.25 = bf16[512,256]{1,0:T(8,128)(2,1)S(1)} collective-permute-done((bf16[512,256]{1,0:T(8,128)(2,1)S(1)}, bf16[512,256]{1,0:T(8,128)(2,1)S(1)}, u32[]{:S(2)}, u32[]{:S(2)}) %collective-permute-start.25) | collective-permute-done | bytes 262176 | tf_op jit(solution)/shard_map/ppermute | solution.py:197
  312.7 20.5 %attn_bwd.1 = bf16[2048,768]{1,0:T(8,128)(2,1)} custom-call(s32[1]{0:T(128)} %bitcast.2.t_ref, bf16[2048,768]{1,0:T(8,128)(2,1)} %pad_maximum_fusion.3.qkv_ref, bf16[2048,256]{1,0:T(8,128)(2,1)} %pad_maximum_fusion.5.do_ref, bf16[2048,256]{1,0:T(8,128)(2,1)} %get-tuple-element.14.o_ref, bf16[2,2048,128]{2,1,0:T(8,128)(2,1)} %get-tuple-element.15.qx_ref, ...), custom_call_target="tpu_custom_call" | custom-call | flops 14000000000 | bytes 24000000 | tf_op jit(solution)/shard_map/attn_bwd/pallas_call | solution.py:160
  333.3 5.9 %fusion.79 = f32[1024,768]{1,0:T(8,128)S(1)} fusion(bf16[2048,768]{1,0:T(8,128)(2,1)} %attn_bwd.1, bf16[512,1024]{1,0:T(8,128)(2,1)S(1)} %copy-done.42, bf16[512,1024]{1,0:T(8,128)(2,1)} %collective-permute-done.1, bf16[512,1024]{1,0:T(8,128)(2,1)S(1)} %copy-done.40, bf16[512,1024]{1,0:T(8,128)(2,1)S(1)} %copy-done.23), kind=kOutput, calls=%fused_computation.206 | convolution fusion | flops 3238002688 | bytes 10485760 | tf_op jit(solution)/shard_map/dot_general | solution.py:25
  342.8 5.6 %convolution_convert_fusion = bf16[2048,1024]{1,0:T(8,128)(2,1)S(1)} fusion(bf16[2048,768]{1,0:T(8,128)(2,1)} %attn_bwd.1, bf16[1024,256]{1,0:T(8,128)(2,1)} %get-tuple-element.84, bf16[1024,256]{1,0:T(8,128)(2,1)} %get-tuple-element.85, bf16[1024,256]{1,0:T(8,128)(2,1)S(1)} %copy-done.24), kind=kOutput, calls=%fused_computation.13 | convolution fusion | flops 3228041216 | bytes 8912896 | tf_op jit(solution)/shard_map/dot_general | solution.py:25
  348.4 2.0 copy-done.9
  352.1 2.0 add_convert_fusion.4
  364.6 4.0 collective-permute-done.35
  371.2 1.9 add_convert_fusion
  375.0 6.2 %collective-permute-done.36 = bf16[2,2,256,128]{3,2,1,0:T(8,128)(2,1)S(1)} collective-permute-done((bf16[2,2,256,128]{3,2,1,0:T(8,128)(2,1)S(1)}, bf16[2,2,256,128]{3,2,1,0:T(8,128)(2,1)S(1)}, u32[]{:S(2)}, u32[]{:S(2)}) %collective-permute-start.36) | collective-permute-done | bytes 262176 | tf_op jit(solution)/shard_map/ppermute | solution.py:229
  383.9 2.7 collective-permute-start.32
  386.5 8.6 %collective-permute-done.37 = bf16[2,256,128]{2,1,0:T(8,128)(2,1)S(1)} collective-permute-done((bf16[2,256,128]{2,1,0:T(8,128)(2,1)S(1)}, bf16[2,256,128]{2,1,0:T(8,128)(2,1)S(1)}, u32[]{:S(2)}, u32[]{:S(2)}) %collective-permute-start.37) | collective-permute-done | bytes 131104 | tf_op jit(solution)/shard_map/ppermute | solution.py:229
  399.0 2.8 fusion.23
  408.9 3.4 collective-permute-done.47
  413.2 2.8 collective-permute-done.48
  416.6 4.9 %fusion.22 = f32[1,512,1024]{2,1,0:T(8,128)} fusion(f32[512,1024]{1,0:T(8,128)} %copy-done.7, bf16[1,512,1024]{2,1,0:T(8,128)(2,1)S(1)} %copy-done.5, f32[512]{0:T(512)S(1)} %broadcast_multiply_fusion, f32[512]{0:T(512)S(1)} %broadcast_multiply_fusion.1, f32[1024]{0:T(1024)S(1)} %copy-done.30, f32[512]{0:T(512)S(1)} %copy-done.33, f32[512]{0:T(512)S(1)} %copy-done.29, ...), kind=kLoop, calls=%fused_computation.37 | loop fusion | flops 7340032 | bytes 8400896 | tf_op jit(solution)/shard_map/broadcast_in_dim | solution.py:352
  (278 shorter events, 88.2 us)
Async XLA Ops:
  0.7 11.9 %collective-permute-start.4 = (s32[512]{0:T(512)}, s32[512]{0:T(512)S(1)}, u32[]{:S(2)}, u32[]{:S(2)}) collective-permute-start(s32[512]{0:T(512)} %bitcast.200), channel_id=1, source_target_pairs={{0,2},{1,3},{2,0},{3,1},{4,6},{5,7},{6,4},{7,5},{8,10},{9,11},{10,... | collective-permute-start | bytes 6152 | tf_op jit(solution)/shard_map/ppermute | solution.py:197
  3.7 8.9 %collective-permute-start.3 = (s32[512]{0:T(512)}, s32[512]{0:T(512)S(1)}, u32[]{:S(2)}, u32[]{:S(2)}) collective-permute-start(s32[512]{0:T(512)} %bitcast.201), channel_id=1, source_target_pairs={{0,1},{1,0},{2,3},{3,2},{4,5},{5,4},{6,7},{7,6},{8,9},{9,8},{10,11... | collective-permute-start | bytes 6152 | tf_op jit(solution)/shard_map/ppermute | solution.py:193
  3.7 67.4 %collective-permute-start.9 = (bf16[256,1024]{1,0:T(8,128)(2,1)}, bf16[256,1024]{1,0:T(8,128)(2,1)}, u32[]{:S(2)}, u32[]{:S(2)}) collective-permute-start(bf16[256,1024]{1,0:T(8,128)(2,1)} %param.16), channel_id=1, source_target_pairs={{0,1},{1,0},{2,3},{3,2},{4,5},{5,4},{6,7},{7,6},{8,9},{9,8},{10,11... | collective-permute-start | bytes 1572872 | tf_op jit(solution)/shard_map/ppermute | solution.py:193
  4.2 41.0 %collective-permute-start.10 = (bf16[256,1024]{1,0:T(8,128)(2,1)}, bf16[256,1024]{1,0:T(8,128)(2,1)}, u32[]{:S(2)}, u32[]{:S(2)}) collective-permute-start(bf16[256,1024]{1,0:T(8,128)(2,1)} %param.16), channel_id=1, source_target_pairs={{0,2},{1,3},{2,0},{3,1},{4,6},{5,7},{6,4},{7,5},{8,10},{9,11},{10,... | collective-permute-start | bytes 1572872 | tf_op jit(solution)/shard_map/ppermute | solution.py:197
  9.1 31.7 %collective-permute-start.1 = (bf16[512,1024]{1,0:T(8,128)(2,1)S(1)}, bf16[512,1024]{1,0:T(8,128)(2,1)}, u32[]{:S(2)}, u32[]{:S(2)}) collective-permute-start(bf16[512,1024]{1,0:T(8,128)(2,1)S(1)} %fusion.17), channel_id=1, source_target_pairs={{0,2},{1,3},{2,0},{3,1},{4,6},{5,7},{6,4},{7,5},{8,10},{9,11},{10,... | collective-permute-start | bytes 3145736 | tf_op jit(solution)/shard_map/ppermute | solution.py:197
  12.6 33.1 %collective-permute-start = (bf16[512,1024]{1,0:T(8,128)(2,1)S(1)}, bf16[512,1024]{1,0:T(8,128)(2,1)S(1)}, u32[]{:S(2)}, u32[]{:S(2)}) collective-permute-start(bf16[512,1024]{1,0:T(8,128)(2,1)S(1)} %fusion.17), channel_id=1, source_target_pairs={{0,1},{1,0},{2,3},{3,2},{4,5},{5,4},{6,7},{7,6},{8,9},{9,8},{10,11... | collective-permute-start | bytes 3145736 | tf_op jit(solution)/shard_map/ppermute | solution.py:193
  40.8 4.9 %collective-permute-start.2 = (bf16[512,1024]{1,0:T(8,128)(2,1)}, bf16[512,1024]{1,0:T(8,128)(2,1)S(1)}, u32[]{:S(2)}, u32[]{:S(2)}) collective-permute-start(bf16[512,1024]{1,0:T(8,128)(2,1)} %collective-permute-done.1), channel_id=1, source_target_pairs={{0,1},{1,0},{2,3},{3,2},{4,5},{5,4},{6,7},{7,6},{8,9},{9,8},{10,11... | collective-permute-start | bytes 3145736 | tf_op jit(solution)/shard_map/ppermute | solution.py:193
  45.2 28.1 %collective-permute-start.11 = (bf16[256,1024]{1,0:T(8,128)(2,1)}, bf16[256,1024]{1,0:T(8,128)(2,1)S(1)}, u32[]{:S(2)}, u32[]{:S(2)}) collective-permute-start(bf16[256,1024]{1,0:T(8,128)(2,1)} %collective-permute-done.10), channel_id=1, source_target_pairs={{0,1},{1,0},{2,3},{3,2},{4,5},{5,4},{6,7},{7,6},{8,9},{9,8},{10,11... | collective-permute-start | bytes 1572872 | tf_op jit(solution)/shard_map/ppermute | solution.py:193
  69.2 8.5 %collective-permute-start.8 = (bf16[512,256]{1,0:T(8,128)(2,1)S(1)}, bf16[512,256]{1,0:T(8,128)(2,1)S(1)}, u32[]{:S(2)}, u32[]{:S(2)}) collective-permute-start(bf16[512,256]{1,0:T(8,128)(2,1)S(1)} %get-tuple-element.92), channel_id=1, source_target_pairs={{0,3},{1,2},{2,1},{3,0},{4,7},{5,6},{6,5},{7,4},{8,11},{9,10},{10,... | collective-permute-start | bytes 786440 | tf_op jit(solution)/shard_map/ppermute | solution.py:201
  69.3 14.2 %collective-permute-start.7 = (bf16[512,256]{1,0:T(8,128)(2,1)S(1)}, bf16[512,256]{1,0:T(8,128)(2,1)S(1)}, u32[]{:S(2)}, u32[]{:S(2)}) collective-permute-start(bf16[512,256]{1,0:T(8,128)(2,1)S(1)} %get-tuple-element.93), channel_id=1, source_target_pairs={{0,2},{1,3},{2,0},{3,1},{4,6},{5,7},{6,4},{7,5},{8,10},{9,11},{10,... | collective-permute-start | bytes 786440 | tf_op jit(solution)/shard_map/ppermute | solution.py:197
  70.9 12.6 %collective-permute-start.6 = (bf16[512,256]{1,0:T(8,128)(2,1)S(1)}, bf16[512,256]{1,0:T(8,128)(2,1)S(1)}, u32[]{:S(2)}, u32[]{:S(2)}) collective-permute-start(bf16[512,256]{1,0:T(8,128)(2,1)S(1)} %get-tuple-element.94), channel_id=1, source_target_pairs={{0,1},{1,0},{2,3},{3,2},{4,5},{5,4},{6,7},{7,6},{8,9},{9,8},{10,11... | collective-permute-start | bytes 786440 | tf_op jit(solution)/shard_map/ppermute | solution.py:193
  86.8 26.4 %collective-permute-start.13 = (bf16[512,1024]{1,0:T(8,128)(2,1)}, bf16[512,1024]{1,0:T(8,128)(2,1)}, u32[]{:S(2)}, u32[]{:S(2)}) collective-permute-start(bf16[512,1024]{1,0:T(8,128)(2,1)} %add_convert_fusion.3), channel_id=1, source_target_pairs={{0,2},{1,3},{2,0},{3,1},{4,6},{5,7},{6,4},{7,5},{8,10},{9,11},{10,... | collective-permute-start | bytes 3145736 | tf_op jit(solution)/shard_map/ppermute | solution.py:197
  88.3 46.2 %collective-permute-start.19 = (bf16[512,1024]{1,0:T(8,128)(2,1)}, bf16[512,1024]{1,0:T(8,128)(2,1)}, u32[]{:S(2)}, u32[]{:S(2)}) collective-permute-start(bf16[512,1024]{1,0:T(8,128)(2,1)} %fusion.28), channel_id=1, source_target_pairs={{0,2},{1,3},{2,0},{3,1},{4,6},{5,7},{6,4},{7,5},{8,10},{9,11},{10,... | collective-permute-start | bytes 3145736 | tf_op jit(solution)/shard_map/ppermute | solution.py:197
  90.0 44.5 %collective-permute-start.12 = (bf16[512,1024]{1,0:T(8,128)(2,1)}, bf16[512,1024]{1,0:T(8,128)(2,1)}, u32[]{:S(2)}, u32[]{:S(2)}) collective-permute-start(bf16[512,1024]{1,0:T(8,128)(2,1)} %add_convert_fusion.3), channel_id=1, source_target_pairs={{0,1},{1,0},{2,3},{3,2},{4,5},{5,4},{6,7},{7,6},{8,9},{9,8},{10,11... | collective-permute-start | bytes 3145736 | tf_op jit(solution)/shard_map/ppermute | solution.py:193
  113.1 21.4 %collective-permute-start.14 = (bf16[512,1024]{1,0:T(8,128)(2,1)}, bf16[512,1024]{1,0:T(8,128)(2,1)}, u32[]{:S(2)}, u32[]{:S(2)}) collective-permute-start(bf16[512,1024]{1,0:T(8,128)(2,1)} %collective-permute-done.13), channel_id=1, source_target_pairs={{0,1},{1,0},{2,3},{3,2},{4,5},{5,4},{6,7},{7,6},{8,9},{9,8},{10,11... | collective-permute-start | bytes 3145736 | tf_op jit(solution)/shard_map/ppermute | solution.py:193
  113.1 36.2 %collective-permute-start.18 = (bf16[512,1024]{1,0:T(8,128)(2,1)}, bf16[512,1024]{1,0:T(8,128)(2,1)}, u32[]{:S(2)}, u32[]{:S(2)}) collective-permute-start(bf16[512,1024]{1,0:T(8,128)(2,1)} %fusion.28), channel_id=1, source_target_pairs={{0,1},{1,0},{2,3},{3,2},{4,5},{5,4},{6,7},{7,6},{8,9},{9,8},{10,11... | collective-permute-start | bytes 3145736 | tf_op jit(solution)/shard_map/ppermute | solution.py:193
  134.5 14.8 %collective-permute-start.20 = (bf16[512,1024]{1,0:T(8,128)(2,1)}, bf16[512,1024]{1,0:T(8,128)(2,1)S(1)}, u32[]{:S(2)}, u32[]{:S(2)}) collective-permute-start(bf16[512,1024]{1,0:T(8,128)(2,1)} %collective-permute-done.19), channel_id=1, source_target_pairs={{0,1},{1,0},{2,3},{3,2},{4,5},{5,4},{6,7},{7,6},{8,9},{9,8},{10,11... | collective-permute-start | bytes 3145736 | tf_op jit(solution)/shard_map/ppermute | solution.py:193
  165.5 31.2 %collective-permute-start.42 = (bf16[2,2,1024,128]{3,2,1,0:T(8,128)(2,1)S(1)}, bf16[2,2,1024,128]{3,2,1,0:T(8,128)(2,1)S(1)}, u32[]{:S(2)}, u32[]{:S(2)}) collective-permute-start(bf16[2,2,1024,128]{3,2,1,0:T(8,128)(2,1)S(1)} %fusion.35), channel_id=1, source_target_pairs={{0,8},{4,12},{8,0},{12,4},{16,24},{20,28},{24,16},{28,20},{1,9},{5... | collective-permute-start | bytes 3145736 | tf_op jit(solution)/shard_map/ppermute | solution.py:229
  187.2 25.4 %collective-permute-start.39 = (bf16[2,2,128,1024]{3,2,0,1:T(8,128)(2,1)S(1)}, bf16[2,2,128,1024]{3,2,0,1:T(8,128)(2,1)S(1)}, u32[]{:S(2)}, u32[]{:S(2)}) collective-permute-start(bf16[2,2,128,1024]{3,2,0,1:T(8,128)(2,1)S(1)} %fusion.36), channel_id=1, source_target_pairs={{0,4},{4,0},{8,12},{12,8},{16,20},{20,16},{24,28},{28,24},{1,5},{5... | collective-permute-start | bytes 3145736 | tf_op jit(solution)/shard_map/ppermute | solution.py:229
  193.9 21.7 %collective-permute-start.22 = (bf16[512,1024]{1,0:T(8,128)(2,1)S(1)}, bf16[512,1024]{1,0:T(8,128)(2,1)S(1)}, u32[]{:S(2)}, u32[]{:S(2)}) collective-permute-start(bf16[512,1024]{1,0:T(8,128)(2,1)S(1)} %get-tuple-element.77), channel_id=1, source_target_pairs={{0,1},{1,0},{2,3},{3,2},{4,5},{5,4},{6,7},{7,6},{8,9},{9,8},{10,11... | collective-permute-start | bytes 3145736 | tf_op jit(solution)/shard_map/ppermute | solution.py:193
  196.1 69.1 %collective-permute-start.15 = (bf16[512,1024]{1,0:T(8,128)(2,1)S(1)}, bf16[512,1024]{1,0:T(8,128)(2,1)S(1)}, u32[]{:S(2)}, u32[]{:S(2)}) collective-permute-start(bf16[512,1024]{1,0:T(8,128)(2,1)S(1)} %get-tuple-element.78), channel_id=1, source_target_pairs={{0,1},{1,0},{2,3},{3,2},{4,5},{5,4},{6,7},{7,6},{8,9},{9,8},{10,11... | collective-permute-start | bytes 3145736 | tf_op jit(solution)/shard_map/ppermute | solution.py:193
  196.2 45.3 %collective-permute-start.16 = (bf16[512,1024]{1,0:T(8,128)(2,1)S(1)}, bf16[512,1024]{1,0:T(8,128)(2,1)S(1)}, u32[]{:S(2)}, u32[]{:S(2)}) collective-permute-start(bf16[512,1024]{1,0:T(8,128)(2,1)S(1)} %get-tuple-element.79), channel_id=1, source_target_pairs={{0,1},{1,0},{2,3},{3,2},{4,5},{5,4},{6,7},{7,6},{8,9},{9,8},{10,11... | collective-permute-start | bytes 3145736 | tf_op jit(solution)/shard_map/ppermute | solution.py:193
  196.7 58.0 %collective-permute-start.21 = (bf16[512,1024]{1,0:T(8,128)(2,1)S(1)}, bf16[512,1024]{1,0:T(8,128)(2,1)S(1)}, u32[]{:S(2)}, u32[]{:S(2)}) collective-permute-start(bf16[512,1024]{1,0:T(8,128)(2,1)S(1)} %get-tuple-element.76), channel_id=1, source_target_pairs={{0,1},{1,0},{2,3},{3,2},{4,5},{5,4},{6,7},{7,6},{8,9},{9,8},{10,11... | collective-permute-start | bytes 3145736 | tf_op jit(solution)/shard_map/ppermute | solution.py:193
  212.6 25.4 %collective-permute-start.43 = (bf16[2,1024,128]{2,1,0:T(8,128)(2,1)S(1)}, bf16[2,1024,128]{2,1,0:T(8,128)(2,1)S(1)}, u32[]{:S(2)}, u32[]{:S(2)}) collective-permute-start(bf16[2,1024,128]{2,1,0:T(8,128)(2,1)S(1)} %fusion.42), channel_id=1, source_target_pairs={{0,16},{4,20},{8,24},{12,28},{16,0},{20,4},{24,8},{28,12},{1,17},{... | collective-permute-start | bytes 1572872 | tf_op jit(solution)/shard_map/ppermute | solution.py:229
  215.7 24.2 %collective-permute-start.40 = (bf16[2,128,1024]{2,1,0:T(8,128)(2,1)S(1)}, bf16[2,128,1024]{2,1,0:T(8,128)(2,1)S(1)}, u32[]{:S(2)}, u32[]{:S(2)}) collective-permute-start(bf16[2,128,1024]{2,1,0:T(8,128)(2,1)S(1)} %fusion.41), channel_id=1, source_target_pairs={{0,8},{4,12},{8,0},{12,4},{16,24},{20,28},{24,16},{28,20},{1,9},{5... | collective-permute-start | bytes 1572872 | tf_op jit(solution)/shard_map/ppermute | solution.py:229
  237.9 26.0 %collective-permute-start.23 = (bf16[512,1024]{1,0:T(8,128)(2,1)S(1)}, bf16[512,1024]{1,0:T(8,128)(2,1)S(1)}, u32[]{:S(2)}, u32[]{:S(2)}) collective-permute-start(bf16[512,1024]{1,0:T(8,128)(2,1)S(1)} %add_convert_fusion.1), channel_id=1, source_target_pairs={{0,2},{1,3},{2,0},{3,1},{4,6},{5,7},{6,4},{7,5},{8,10},{9,11},{10,... | collective-permute-start | bytes 3145736 | tf_op jit(solution)/shard_map/ppermute | solution.py:197
  239.9 6.7 %collective-permute-start.44 = (bf16[1024,128]{1,0:T(8,128)(2,1)S(1)}, bf16[1024,128]{1,0:T(8,128)(2,1)S(1)}, u32[]{:S(2)}, u32[]{:S(2)}) collective-permute-start(bf16[1024,128]{1,0:T(8,128)(2,1)S(1)} %fusion.48), channel_id=1, source_target_pairs={{0,4},{4,0},{8,12},{12,8},{16,20},{20,16},{24,28},{28,24},{1,5},{5... | collective-permute-start | bytes 786440 | tf_op jit(solution)/shard_map/ppermute | solution.py:229
  241.6 12.3 %collective-permute-start.41 = (bf16[128,1024]{1,0:T(8,128)(2,1)S(1)}, bf16[128,1024]{1,0:T(8,128)(2,1)S(1)}, u32[]{:S(2)}, u32[]{:S(2)}) collective-permute-start(bf16[128,1024]{1,0:T(8,128)(2,1)S(1)} %fusion.47), channel_id=1, source_target_pairs={{0,16},{4,20},{8,24},{12,28},{16,0},{20,4},{24,8},{28,12},{1,17},{... | collective-permute-start | bytes 786440 | tf_op jit(solution)/shard_map/ppermute | solution.py:229
  246.5 38.9 %collective-permute-start.17 = (bf16[512,1024]{1,0:T(8,128)(2,1)S(1)}, bf16[512,1024]{1,0:T(8,128)(2,1)S(1)}, u32[]{:S(2)}, u32[]{:S(2)}) collective-permute-start(bf16[512,1024]{1,0:T(8,128)(2,1)S(1)} %add_convert_fusion.2), channel_id=1, source_target_pairs={{0,2},{1,3},{2,0},{3,1},{4,6},{5,7},{6,4},{7,5},{8,10},{9,11},{10,... | collective-permute-start | bytes 3145736 | tf_op jit(solution)/shard_map/ppermute | solution.py:197
  298.7 8.6 %collective-permute-start.26 = (bf16[512,256]{1,0:T(8,128)(2,1)S(1)}, bf16[512,256]{1,0:T(8,128)(2,1)S(1)}, u32[]{:S(2)}, u32[]{:S(2)}) collective-permute-start(bf16[512,256]{1,0:T(8,128)(2,1)S(1)} %bitcast.195), channel_id=1, source_target_pairs={{0,3},{1,2},{2,1},{3,0},{4,7},{5,6},{6,5},{7,4},{8,11},{9,10},{10,... | collective-permute-start | bytes 786440 | tf_op jit(solution)/shard_map/ppermute | solution.py:201
  298.8 8.6 %collective-permute-start.24 = (bf16[512,256]{1,0:T(8,128)(2,1)S(1)}, bf16[512,256]{1,0:T(8,128)(2,1)S(1)}, u32[]{:S(2)}, u32[]{:S(2)}) collective-permute-start(bf16[512,256]{1,0:T(8,128)(2,1)S(1)} %bitcast.194), channel_id=1, source_target_pairs={{0,1},{1,0},{2,3},{3,2},{4,5},{5,4},{6,7},{7,6},{8,9},{9,8},{10,11... | collective-permute-start | bytes 786440 | tf_op jit(solution)/shard_map/ppermute | solution.py:193
  299.4 12.2 %collective-permute-start.25 = (bf16[512,256]{1,0:T(8,128)(2,1)S(1)}, bf16[512,256]{1,0:T(8,128)(2,1)S(1)}, u32[]{:S(2)}, u32[]{:S(2)}) collective-permute-start(bf16[512,256]{1,0:T(8,128)(2,1)S(1)} %bitcast.193), channel_id=1, source_target_pairs={{0,2},{1,3},{2,0},{3,1},{4,6},{5,7},{6,4},{7,5},{8,10},{9,11},{10,... | collective-permute-start | bytes 786440 | tf_op jit(solution)/shard_map/ppermute | solution.py:197
  305.8 58.8 %collective-permute-start.33 = (bf16[256,1024]{0,1:T(8,128)(2,1)}, bf16[256,1024]{0,1:T(8,128)(2,1)S(1)}, u32[]{:S(2)}, u32[]{:S(2)}) collective-permute-start(bf16[256,1024]{0,1:T(8,128)(2,1)} %get-tuple-element.81), channel_id=1, source_target_pairs={{0,1},{1,0},{2,3},{3,2},{4,5},{5,4},{6,7},{7,6},{8,9},{9,8},{10,11... | collective-permute-start | bytes 1572872 | tf_op jit(solution)/shard_map/ppermute | solution.py:193
  305.8 46.3 %collective-permute-start.34 = (bf16[256,1024]{0,1:T(8,128)(2,1)}, bf16[256,1024]{0,1:T(8,128)(2,1)S(1)}, u32[]{:S(2)}, u32[]{:S(2)}) collective-permute-start(bf16[256,1024]{0,1:T(8,128)(2,1)} %get-tuple-element.82), channel_id=1, source_target_pairs={{0,1},{1,0},{2,3},{3,2},{4,5},{5,4},{6,7},{7,6},{8,9},{9,8},{10,11... | collective-permute-start | bytes 1572872 | tf_op jit(solution)/shard_map/ppermute | solution.py:193
  341.2 20.1 %collective-permute-start.30 = (bf16[2,2,128,768]{2,3,0,1:T(8,128)(2,1)S(1)}, bf16[2,2,128,768]{2,3,0,1:T(8,128)(2,1)}, u32[]{:S(2)}, u32[]{:S(2)}) collective-permute-start(bf16[2,2,128,768]{2,3,0,1:T(8,128)(2,1)S(1)} %bitcast.192), channel_id=1, source_target_pairs={{0,4},{4,0},{8,12},{12,8},{16,20},{20,16},{24,28},{28,24},{1,5},{5... | collective-permute-start | bytes 2359304 | tf_op jit(solution)/shard_map/ppermute | solution.py:229
  351.9 18.4 %collective-permute-start.28 = (bf16[512,1024]{1,0:T(8,128)(2,1)}, bf16[512,1024]{1,0:T(8,128)(2,1)}, u32[]{:S(2)}, u32[]{:S(2)}) collective-permute-start(bf16[512,1024]{1,0:T(8,128)(2,1)} %get-tuple-element.75), channel_id=1, source_target_pairs={{0,1},{1,0},{2,3},{3,2},{4,5},{5,4},{6,7},{7,6},{8,9},{9,8},{10,11... | collective-permute-start | bytes 3145736 | tf_op jit(solution)/shard_map/ppermute | solution.py:193
  354.1 14.5 %collective-permute-start.35 = (bf16[256,1024]{0,1:T(8,128)(2,1)}, bf16[256,1024]{0,1:T(8,128)(2,1)S(1)}, u32[]{:S(2)}, u32[]{:S(2)}) collective-permute-start(bf16[256,1024]{0,1:T(8,128)(2,1)} %add_convert_fusion.4), channel_id=1, source_target_pairs={{0,2},{1,3},{2,0},{3,1},{4,6},{5,7},{6,4},{7,5},{8,10},{9,11},{10,... | collective-permute-start | bytes 1572872 | tf_op jit(solution)/shard_map/ppermute | solution.py:197
  359.4 37.3 %collective-permute-start.27 = (bf16[512,1024]{1,0:T(8,128)(2,1)}, bf16[512,1024]{1,0:T(8,128)(2,1)}, u32[]{:S(2)}, u32[]{:S(2)}) collective-permute-start(bf16[512,1024]{1,0:T(8,128)(2,1)} %get-tuple-element.74), channel_id=1, source_target_pairs={{0,1},{1,0},{2,3},{3,2},{4,5},{5,4},{6,7},{7,6},{8,9},{9,8},{10,11... | collective-permute-start | bytes 3145736 | tf_op jit(solution)/shard_map/ppermute | solution.py:193
  364.6 18.1 %collective-permute-start.31 = (bf16[2,128,768]{1,2,0:T(8,128)(2,1)}, bf16[2,128,768]{1,2,0:T(8,128)(2,1)}, u32[]{:S(2)}, u32[]{:S(2)}) collective-permute-start(bf16[2,128,768]{1,2,0:T(8,128)(2,1)} %fusion.45), channel_id=1, source_target_pairs={{0,8},{4,12},{8,0},{12,4},{16,24},{20,28},{24,16},{28,20},{1,9},{5... | collective-permute-start | bytes 1179656 | tf_op jit(solution)/shard_map/ppermute | solution.py:229
  370.2 11.0 %collective-permute-start.36 = (bf16[2,2,256,128]{3,2,1,0:T(8,128)(2,1)S(1)}, bf16[2,2,256,128]{3,2,1,0:T(8,128)(2,1)S(1)}, u32[]{:S(2)}, u32[]{:S(2)}) collective-permute-start(bf16[2,2,256,128]{3,2,1,0:T(8,128)(2,1)S(1)} %fusion.46), channel_id=1, source_target_pairs={{0,8},{4,12},{8,0},{12,4},{16,24},{20,28},{24,16},{28,20},{1,9},{5... | collective-permute-start | bytes 786440 | tf_op jit(solution)/shard_map/ppermute | solution.py:229
  373.2 24.8 %collective-permute-start.29 = (bf16[512,1024]{1,0:T(8,128)(2,1)S(1)}, bf16[512,1024]{1,0:T(8,128)(2,1)S(1)}, u32[]{:S(2)}, u32[]{:S(2)}) collective-permute-start(bf16[512,1024]{1,0:T(8,128)(2,1)S(1)} %add_convert_fusion), channel_id=1, source_target_pairs={{0,2},{1,3},{2,0},{3,1},{4,6},{5,7},{6,4},{7,5},{8,10},{9,11},{10,... | collective-permute-start | bytes 3145736 | tf_op jit(solution)/shard_map/ppermute | solution.py:197
  382.3 12.7 %collective-permute-start.37 = (bf16[2,256,128]{2,1,0:T(8,128)(2,1)S(1)}, bf16[2,256,128]{2,1,0:T(8,128)(2,1)S(1)}, u32[]{:S(2)}, u32[]{:S(2)}) collective-permute-start(bf16[2,256,128]{2,1,0:T(8,128)(2,1)S(1)} %fusion.50), channel_id=1, source_target_pairs={{0,16},{4,20},{8,24},{12,28},{16,0},{20,4},{24,8},{28,12},{1,17},{... | collective-permute-start | bytes 393224 | tf_op jit(solution)/shard_map/ppermute | solution.py:229
  383.9 22.6 %collective-permute-start.32 = (bf16[128,768]{0,1:T(8,128)(2,1)S(1)}, bf16[128,768]{0,1:T(8,128)(2,1)S(1)}, u32[]{:S(2)}, u32[]{:S(2)}) collective-permute-start(bf16[128,768]{0,1:T(8,128)(2,1)S(1)} %fusion.49), channel_id=1, source_target_pairs={{0,16},{4,20},{8,24},{12,28},{16,0},{20,4},{24,8},{28,12},{1,17},{... | collective-permute-start | bytes 589832 | tf_op jit(solution)/shard_map/ppermute | solution.py:229
  395.1 8.7 %collective-permute-start.38 = (bf16[256,128]{1,0:T(8,128)(2,1)S(1)}, bf16[256,128]{1,0:T(8,128)(2,1)S(1)}, u32[]{:S(2)}, u32[]{:S(2)}) collective-permute-start(bf16[256,128]{1,0:T(8,128)(2,1)S(1)} %fusion.51), channel_id=1, source_target_pairs={{0,4},{4,0},{8,12},{12,8},{16,20},{20,16},{24,28},{28,24},{1,5},{5... | collective-permute-start | bytes 196616 | tf_op jit(solution)/shard_map/ppermute | solution.py:229
  402.2 4.2 collective-permute-start.45
  407.6 4.7 %collective-permute-start.47 = (f32[2,2,6,32]{3,1,2,0:T(2,128)S(1)}, f32[2,2,6,32]{3,1,2,0:T(2,128)S(1)}, u32[]{:S(2)}, u32[]{:S(2)}) collective-permute-start(f32[2,2,6,32]{3,1,2,0:T(2,128)S(1)} %bitcast.199), channel_id=1, source_target_pairs={{0,16},{4,20},{8,24},{12,28},{16,0},{20,4},{24,8},{28,12},{1,17},{... | collective-permute-start | bytes 9224 | tf_op jit(solution)/shard_map/ppermute | solution.py:347
  412.3 3.7 collective-permute-start.48
  416.1 5.4 %collective-permute-start.49 = (f32[6,32]{1,0:T(8,128)S(1)}, f32[6,32]{1,0:T(8,128)S(1)}, u32[]{:S(2)}, u32[]{:S(2)}) collective-permute-start(f32[6,32]{1,0:T(8,128)S(1)} %bitcast.204), channel_id=1, source_target_pairs={{0,4},{4,0},{8,12},{12,8},{16,20},{20,16},{24,28},{28,24},{1,5},{5... | collective-permute-start | bytes 2312 | tf_op jit(solution)/shard_map/ppermute | solution.py:347
  (51 other events, 695.0 us)
